TPU v7x, 128 devices: a whole 4x4x4 slice. The times are simulated.
128 devices in a mesh: dp: 2 (over core), tile: 64 (over y, z, x).
Axes of the slice: x: 4, y: 4, z: 4, core: 2. Of those that a mesh axis runs over, the one named last changes fastest.
Arguments:
- tile_latents: bfloat16 [6016, 4096], P(('dp', 'tile')), parts along dimension 0, may hold values from -6 to 6
- tile_owner: int32 [6016], P(('dp', 'tile')), parts along dimension 0, may hold values from -1 to 63, as said below
- tile_position: int32 [6016], P(('dp', 'tile')), parts along dimension 0, may hold values from -1 to 23, as said below
- neighbour_owner: int32 [3072, 8], P(('dp', 'tile')), parts along dimension 0, may hold values from -1 to 63, as said below
- neighbour_slot: int32 [3072, 8], P(('dp', 'tile')), parts along dimension 0, may hold values from -1 to 23, as said below
- w_embed: bfloat16 [64, 2048], replicated, may hold values from -0.75 to 0.75
- norm_gain: float32 [2048], replicated, may hold values from 0.1 to 1.9
- w_query: bfloat16 [2048, 1024], replicated
- w_key: bfloat16 [2048, 1024], replicated
- w_value: bfloat16 [2048, 1024], replicated, may hold values from -0.125 to 0.125
- w_out: bfloat16 [1024, 2048], replicated, may hold values from -0.1875 to 0.1875
Outputs:
- mixed: bfloat16 [196608, 2048], P(('dp', 'tile')), parts along dimension 0
There are 2 independent parts, one for each index of `dp`. A program takes and returns all parts, laid end to end along the dimension named above; an argument that names none is the same for every part. Nothing has to cross between parts.
Inputs may be any that keep to these rules, and one draw needn't show every extreme that they name: `tile_owner`: -1 marks an empty slot and a loader's live slots come first. Every owner receives exactly one tile for each of its 24 positions, at most 1 from one loader, and that most is reached; some loader fills all 47 slots. Taken loader by loader and slot by slot, the m-th live slot goes to owner (m + r) mod 64 at position m // 64, for one r of the draw. `tile_position`: -1 exactly on empty slots. `neighbour_owner`: rows follow the packed tile order (owner by owner, position by position). Images of at most 13 tiles a row are laid row by row in that order, so a tile's left neighbour is the tile before it and its right neighbour the tile after it. A neighbour on another owner lies on the owner just before or just after; on the next owner it is among the first 14 tiles, on the previous among the last 14, and both ends are reached. -1 marks a neighbour outside the tile's image. `neighbour_slot`: -1 exactly where neighbour_owner is -1.
All inputs are finite; a program needn't handle non-finite values.
Results may differ from a plain program's by a relative error of at most 0.0078.
Values may be sent and summed in bfloat16 or wider, within the bound.
A program may use at most 192 MiB of HBM per device.

v0:
```python
import math

import jax
import jax.numpy as jnp
from jax import lax
from jax.sharding import PartitionSpec as P

HEADS = 8
HEAD = 128
LAT = 64
SIDE = 8
RADIUS = 6
HALO = 14


EPSILON = 1e-06


def with_halo(shard, sides, width):
    for axis, dim in sides:
        devices, length = (lax.axis_size(axis), shard.shape[dim])
        up = [(i, (i + 1) % devices) for i in range(devices - 1)]
        down = [(j, i) for i, j in up]
        last = lax.slice_in_dim(shard, length - width, length, axis=dim)
        initial = lax.slice_in_dim(shard, 0, width, axis=dim)
        before = lax.ppermute(last, axis, up)
        after = lax.ppermute(initial, axis, down)
        shard = jnp.concatenate([before, shard, after], axis=dim)
    return shard


def window_mask():
    tile_tokens = SIDE * SIDE
    query_ids = jnp.arange(tile_tokens)
    key_ids = jnp.arange(9 * tile_tokens)
    region = key_ids // tile_tokens
    within = key_ids % tile_tokens
    offset_rows = (region // 3 - 1) * SIDE + within // SIDE
    offset_cols = (region % 3 - 1) * SIDE + within % SIDE
    offset_rows = offset_rows[None, :] - (query_ids // SIDE)[:, None]
    offset_cols = offset_cols[None, :] - (query_ids % SIDE)[:, None]
    return (jnp.abs(offset_rows) <= RADIUS) & (jnp.abs(offset_cols) <= RADIUS)


def normed_rows(latent_block, w_embed, norm_gain):
    token_rows = latent_block.reshape(-1, LAT)
    embedded = jnp.dot(token_rows, w_embed, preferred_element_type=jnp.float32)
    inverse_rms = lax.rsqrt(jnp.mean(embedded * embedded, axis=-1, keepdims=True) + EPSILON)
    return (embedded * inverse_rms * norm_gain).astype(jnp.bfloat16)


def head_major(normed, weight, tile_count, tile_tokens):
    shaped = weight.reshape(weight.shape[0], HEADS, HEAD)
    projected = jnp.einsum(
        "nc,chd->hnd", normed, shaped, preferred_element_type=jnp.float32
    ).astype(jnp.bfloat16)
    return projected.reshape(HEADS, tile_count, tile_tokens, HEAD)


def key_value(normed, w_key, w_value, tile_count, tile_tokens):
    return jnp.stack(
        [
            head_major(normed, w_key, tile_count, tile_tokens),
            head_major(normed, w_value, tile_count, tile_tokens),
        ],
        axis=0,
    )


def attend_block(query_block, extended, index_block, present, mask_window, w_out):
    group_tiles = query_block.shape[1]
    tile_tokens = query_block.shape[2]
    key_heads = extended[0][:, index_block].reshape(HEADS, group_tiles, 9 * tile_tokens, HEAD)
    value_heads = extended[1][:, index_block].reshape(HEADS, group_tiles, 9 * tile_tokens, HEAD)
    scores = jnp.einsum(
        "hgqd,hgkd->hgqk", query_block, key_heads, preferred_element_type=jnp.float32
    ) * HEAD ** (-0.5)
    allowed = mask_window[None, None] & jnp.repeat(present, tile_tokens, axis=1)[None, :, None, :]
    scores = jnp.where(allowed, scores, -jnp.inf)
    row_max = jnp.max(scores, axis=-1, keepdims=True)
    raised = jnp.where(allowed, jnp.exp(scores - row_max), 0.0)
    totals = jnp.sum(raised, axis=-1)
    weights = raised.astype(jnp.bfloat16)
    summed = jnp.einsum("hgqk,hgkd->hgqd", weights, value_heads, preferred_element_type=jnp.float32)
    attended = (summed / totals[..., None]).astype(jnp.bfloat16)
    out_heads = w_out.reshape(HEADS, HEAD, w_out.shape[1])
    projected = jnp.einsum(
        "hgqd,hde->gqe", attended, out_heads, preferred_element_type=jnp.float32
    ).astype(jnp.bfloat16)
    return projected.reshape(group_tiles * tile_tokens, w_out.shape[1])


def local(
    tile_latents,
    tile_owner,
    tile_position,
    neighbour_owner,
    neighbour_slot,
    w_embed,
    norm_gain,
    w_query,
    w_key,
    w_value,
    w_out,
):
    slot_count = tile_latents.shape[0]
    values = tile_latents.shape[1]
    tile_count = neighbour_owner.shape[0]
    devices = lax.axis_size("tile")
    capacity = -(-slot_count // devices)
    tile_tokens = SIDE * SIDE
    ordering = jnp.arange(slot_count)
    earlier = (tile_owner[:, None] == tile_owner[None, :]) & (ordering[None, :] < ordering[:, None])
    ranked = jnp.sum(earlier.astype(jnp.int32), axis=1)
    target = jnp.where(tile_owner >= 0, tile_owner * capacity + ranked, -1)
    chosen = jnp.arange(devices * capacity)[:, None] == target[None, :]
    outgoing = jnp.dot(
        chosen.astype(jnp.bfloat16), tile_latents, preferred_element_type=jnp.float32
    ).astype(jnp.bfloat16)
    places = jnp.sum(jnp.where(chosen, tile_position[None, :] + 1, 0), axis=1) - 1
    arrived, arrived_spots = (
        lax.all_to_all(
            outgoing.reshape(devices, capacity, values),
            "tile",
            split_axis=0,
            concat_axis=0,
            tiled=True,
        ),
        lax.all_to_all(
            places.reshape(devices, capacity), "tile", split_axis=0, concat_axis=0, tiled=True
        ),
    )
    taken_rows = jnp.arange(tile_count)[:, None] == arrived_spots.reshape(1, -1)
    owned_tiles = jnp.dot(
        taken_rows.astype(jnp.bfloat16),
        arrived.reshape(devices * capacity, values),
        preferred_element_type=jnp.float32,
    ).astype(jnp.bfloat16)
    normed = normed_rows(owned_tiles, w_embed, norm_gain)
    queries = head_major(normed, w_query, tile_count, tile_tokens)
    key_values = key_value(normed, w_key, w_value, tile_count, tile_tokens)
    extended = with_halo(key_values, (("tile", 2),), HALO)
    my_index = lax.axis_index("tile")
    exists = neighbour_owner >= 0
    neighbour_index = jnp.where(
        exists, HALO + (neighbour_owner - my_index) * tile_count + neighbour_slot, 0
    )
    self_index = (HALO + jnp.arange(tile_count, dtype=jnp.int32))[:, None]
    index_nine = jnp.concatenate(
        [neighbour_index[:, :4], self_index, neighbour_index[:, 4:]], axis=1
    )
    present_nine = jnp.concatenate(
        [exists[:, :4], jnp.ones((tile_count, 1), dtype=bool), exists[:, 4:]], axis=1
    )
    mask_window = window_mask()
    group_tiles = math.gcd(tile_count, 8)
    step_count = tile_count // group_tiles

    def attend_step(inputs):
        step_number, index_block, present_block = inputs
        query_block = lax.dynamic_slice_in_dim(queries, step_number * group_tiles, group_tiles, 1)
        return attend_block(query_block, extended, index_block, present_block, mask_window, w_out)

    result = lax.map(
        attend_step,
        (
            jnp.arange(step_count, dtype=jnp.int32),
            index_nine.reshape(step_count, group_tiles, 9),
            present_nine.reshape(step_count, group_tiles, 9),
        ),
    )
    return result.reshape(tile_count * tile_tokens, w_out.shape[1])


def solution(mesh):
    return jax.shard_map(
        local,
        mesh=mesh,
        in_specs=(
            P(("dp", "tile"), None),
            P(("dp", "tile")),
            P(("dp", "tile")),
            P(("dp", "tile"), None),
            P(("dp", "tile"), None),
            P(),
            P(),
            P(),
            P(),
            P(),
            P(),
        ),
        out_specs=P(("dp", "tile"), None),
        check_vma=False,
    )
```

profile of v0, /device:TPU:0, one launch (start us, length us, event | category | flops | bytes accessed | tf_op | source)
XLA Modules:
  0.0 386.8 jit_solution(3454719997193327184)
XLA Ops:
  0.0 0.9 convert_reduce_fusion
  0.9 0.7 compare_select_fusion.1
  1.7 0.7 copy.55
  2.4 11.5 %all-to-all-start = ((s32[64,1,1]{2,1,0:T(1,128)}), s32[64,1,1]{2,1,0:T(1,128)S(1)}, u32[]{:S(2)}, u32[]{:S(2)}) async-start(s32[64,1,1]{2,1,0:T(1,128)} %copy.55), calls=%async_computation | async-start | bytes 65536 | tf_op jit(solution)/shard_map/all_to_all | solution.py:129
  14.9 1.0 reduce.1
  15.9 1.2 reshape.260
  17.0 6.4 %all-to-all-done = s32[64,1,1]{2,1,0:T(1,128)S(1)} async-done(((s32[64,1,1]{2,1,0:T(1,128)}), s32[64,1,1]{2,1,0:T(1,128)S(1)}, u32[]{:S(2)}, u32[]{:S(2)}) %all-to-all-start) | async-done | bytes 288 | tf_op jit(solution)/shard_map/all_to_all | solution.py:129
  23.5 5.1 %all-to-all-start.1 = ((bf16[64,2,2048]{2,1,0:T(2,128)(2,1)}), bf16[64,2,2048]{2,1,0:T(2,128)(2,1)S(1)}, u32[]{:S(2)}, u32[]{:S(2)}) async-start(bf16[64,2,2048]{2,1,0:T(2,128)(2,1)} %reshape.260), calls=%async_computation.1 | async-start | bytes 1048576 | tf_op jit(solution)/shard_map/all_to_all | solution.py:122
  28.6 1.2 reduce
  29.8 10.7 %all-to-all-done.1 = bf16[64,2,2048]{2,1,0:T(2,128)(2,1)S(1)} async-done(((bf16[64,2,2048]{2,1,0:T(2,128)(2,1)}), bf16[64,2,2048]{2,1,0:T(2,128)(2,1)S(1)}, u32[]{:S(2)}, u32[]{:S(2)}) %all-to-all-start.1) | async-done | bytes 524320 | tf_op jit(solution)/shard_map/all_to_all | solution.py:122
  41.0 0.7 convolution_convert_fusion.1
  42.1 6.3 %multiply_reduce_fusion = (f32[1536]{0:T(1024)S(1)}, f32[1536,2048]{1,0:T(8,128)}) fusion(bf16[1536,64]{1,0:T(8,128)(2,1)S(1)} %reshape.221, bf16[64,2048]{1,0:T(8,128)(2,1)S(1)} %copy-done.5), kind=kOutput, calls=%fused_computation.36 | convolution fusion | flops 408943104 | bytes 13047808 | tf_op jit(solution)/shard_map/dot_general | solution.py:47
  48.4 8.3 %fusion.35 = bf16[1536,2048,1]{1,0,2:T(8,128)(2,1)} fusion(f32[1536,2048]{1,0:T(8,128)} %get-tuple-element.179, f32[2048]{0:T(1024)S(1)} %copy-done.9, f32[1536]{0:T(1024)S(1)} %add_rsqrt_fusion), kind=kLoop, calls=%fused_computation.37 | loop fusion | flops 9437184 | bytes 18888704 | tf_op jit(solution)/shard_map/convert_element_type | solution.py:49
  56.7 10.1 %fusion.49 = bf16[1536,8,128]{2,0,1:T(8,128)(2,1)S(1)} fusion(bf16[1536,2048,1]{1,0,2:T(8,128)(2,1)} %fusion.35, bf16[2048,1024]{1,0:T(8,128)(2,1)} %param.21), kind=kOutput, calls=%fused_computation.53 | convolution fusion | flops 6444023808 | bytes 13631488 | tf_op jit(solution)/shard_map/nc,chd->hnd/dot_general | solution.py:54
  66.9 7.1 %fusion.52 = bf16[1536,8,128]{2,0,1:T(8,128)(2,1)S(1)} fusion(bf16[1536,2048,1]{1,0,2:T(8,128)(2,1)S(1)} %copy-done.4, bf16[2048,1024]{1,0:T(8,128)(2,1)S(1)} %copy-done.11), kind=kOutput, calls=%fused_computation.54 | convolution fusion | flops 6444023808 | bytes 13631488 | tf_op jit(solution)/shard_map/nc,chd->hnd/dot_general | solution.py:54
  74.0 3.5 fusion.55
  77.9 4.2 %collective-permute-start = (bf16[2,8,14,64,128]{4,3,2,1,0:T(8,128)(2,1)}, bf16[2,8,14,64,128]{4,3,2,1,0:T(8,128)(2,1)}, u32[]{:S(2)}, u32[]{:S(2)}) collective-permute-start(bf16[2,8,14,64,128]{4,3,2,1,0:T(8,128)(2,1)} %get-tuple-element.172), channel_id=1, source_target_pairs={{0,1},{1,2},{2,3},{3,4},{4,5},{5,6},{6,7},{7,8},{8,9},{9,10},{10,1... | collective-permute-start | bytes 11010056 | tf_op jit(solution)/shard_map/ppermute | solution.py:26
  82.2 1.5 collective-permute-start.1
  84.3 11.3 %fusion.46 = bf16[1536,8,128]{2,0,1:T(8,128)(2,1)} fusion(bf16[1536,2048,1]{1,0,2:T(8,128)(2,1)} %fusion.35, bf16[2048,1024]{1,0:T(8,128)(2,1)} %param.20), kind=kOutput, calls=%fused_computation.52 | convolution fusion | flops 6444023808 | bytes 13631488 | tf_op jit(solution)/shard_map/nc,chd->hnd/dot_general | solution.py:54
  95.7 61.3 %collective-permute-done = bf16[2,8,14,64,128]{4,3,2,1,0:T(8,128)(2,1)} collective-permute-done((bf16[2,8,14,64,128]{4,3,2,1,0:T(8,128)(2,1)}, bf16[2,8,14,64,128]{4,3,2,1,0:T(8,128)(2,1)}, u32[]{:S(2)}, u32[]{:S(2)}) %collective-permute-start) | collective-permute-done | bytes 3670048 | tf_op jit(solution)/shard_map/ppermute | solution.py:26
  156.9 6.0 %collective-permute-done.1 = bf16[2,8,14,64,128]{4,3,2,1,0:T(8,128)(2,1)} collective-permute-done((bf16[2,8,14,64,128]{4,3,2,1,0:T(8,128)(2,1)}, bf16[2,8,14,64,128]{4,3,2,1,0:T(8,128)(2,1)}, u32[]{:S(2)}, u32[]{:S(2)}) %collective-permute-start.1) | collective-permute-done | bytes 3670048 | tf_op jit(solution)/shard_map/ppermute | solution.py:27
  162.9 9.7 %pad_maximum_fusion = bf16[2,8,52,64,128]{4,3,2,1,0:T(8,128)(2,1)} fusion(bf16[2,8,14,64,128]{4,3,2,1,0:T(8,128)(2,1)} %collective-permute-done.1, bf16[1,8,24,64,128]{4,3,2,1,0:T(8,128)(2,1)S(1)} %bitcast.121, bf16[1,8,24,64,128]{4,3,2,1,0:T(8,128)(2,1)S(1)} %bitcast.119, bf16[2,8,14,64,128]{4,3,2,1,0:T(8,128)(2,1)} %collective-permute-done), kind=kLoop, calls=%fused_computation.34 | loop fusion | flops 20447232 | bytes 27262976 | tf_op jit(solution)/shard_map/concatenate | solution.py:28
  172.6 213.2 %while.11 = (s32[]{:T(128)}, bf16[3,512,2048]{2,1,0:T(8,128)(2,1)}, pred[3,8,9]{2,1,0:T(8,128)(4,1)S(1)}, s32[3]{0:T(128)S(1)}, bf16[8,24,64,128]{3,2,1,0:T(8,12...) while((s32[]{:T(128)}, bf16[3,512,2048]{2,1,0:T(8,128)(2,1)}, ...), condition=%wide.region_6.7_spmd.clone, body=%wide.region_3.6_spmd.clone.sunk | while | flops 3372250880 | bytes 143728592 | solution.py:164
  174.5 10.9 %slice_bitcast_fusion.3 = (bf16[8,52,64,128]{3,2,1,0:T(8,128)(2,1)}, bf16[8,52,64,128]{3,2,1,0:T(8,128)(2,1)}) fusion(bf16[2,8,52,64,128]{4,3,2,1,0:T(8,128)(2,1)} %get-tuple-element.304), kind=kLoop, calls=%fused_computation.9.clone.1 | loop fusion | bytes 27262976 | tf_op jit(solution)/shard_map/while/body/eval_jaxpr/squeeze | solution.py:74
  185.4 8.8 %gather_fusion = bf16[72,8,64,128]{3,2,1,0:T(8,128)(2,1)} fusion(bf16[8,52,64,128]{3,2,1,0:T(8,128)(2,1)} %get-tuple-element.263, s32[1024]{0:T(1024)S(1)} %pad_clamp_fusion.2), kind=kCustom, calls=%fused_computation.clone.clone.1 | custom fusion | bytes 18874656 | tf_op jit(solution)/shard_map/while/body/eval_jaxpr/gather | solution.py:73
  194.2 10.6 %copy.108 = bf16[8,8,9,64,128]{4,3,2,1,0:T(8,128)(2,1)} copy(bf16[8,8,9,64,128]{4,3,0,2,1:T(8,128)(2,1)} %bitcast.114) | data formatting | bytes 18874368 | tf_op jit(solution)/shard_map/while/body/eval_jaxpr/gather | solution.py:73
  204.8 9.1 %fusion.119 = (bf16[8,8,64,576]{3,2,1,0:T(8,128)(2,1)}, f32[8,8,64]{2,1,0:T(8,128)S(1)}) fusion(pred[8,64,576]{2,1,0:T(8,128)(4,1)S(1)} %broadcast_and_fusion.2, bf16[8,8,576,128]{3,2,1,0:T(8,128)(2,1)} %bitcast.115, bf16[8,24,64,128]{3,2,1,0:T(8,128)(2,1)} %get-tuple-element.303, s32[]{:T(128)S(6)} %select_n.223), kind=kOutput, calls=%fused_computation.118.clone.1 | convolution fusion | flops 618136128 | bytes 15876100 | tf_op jit(solution)/shard_map/while/body/eval_jaxpr/sub | solution.py:81
  214.0 8.8 %gather_fusion.1 = bf16[72,8,64,128]{3,2,1,0:T(8,128)(2,1)} fusion(bf16[8,52,64,128]{3,2,1,0:T(8,128)(2,1)} %get-tuple-element.265, s32[1024]{0:T(1024)S(1)} %pad_clamp_fusion.2), kind=kCustom, calls=%fused_computation.1.clone.clone.1 | custom fusion | bytes 18874656 | tf_op jit(solution)/shard_map/while/body/eval_jaxpr/gather | solution.py:74
  222.8 10.6 %copy.110 = bf16[72,8,64,128]{3,2,0,1:T(8,128)(2,1)} copy(bf16[72,8,64,128]{3,2,1,0:T(8,128)(2,1)} %gather_fusion.1) | data formatting | bytes 18874368 | tf_op jit(solution)/shard_map/while/body/eval_jaxpr/gather | solution.py:74
  233.4 8.8 %bitcast_convert_fusion.2 = bf16[8,64,2048]{2,1,0:T(8,128)(2,1)S(1)} fusion(bf16[8,128,2048,1]{2,1,0,3:T(8,128)(2,1)} %bitcast.123, f32[8,8,64]{2,0,1:T(8,128)S(1)} %copy.109, bf16[8,8,576,128]{3,2,1,0:T(8,128)(2,1)} %bitcast.116, bf16[8,8,64,576]{3,2,1,0:T(8,128)(2,1)} %get-tuple-element.266), kind=kOutput, calls=%fused_computation.16.clone.1 | convolution fusion | flops 2753560576 | bytes 20463616 | tf_op jit(solution)/shard_map/while/body/eval_jaxpr/hgqd,hde->gqe/dot_general | solution.py:87
  242.2 1.5 bitcast_dynamic-update-slice_fusion.2
  245.6 10.9 %slice_bitcast_fusion.3 = (bf16[8,52,64,128]{3,2,1,0:T(8,128)(2,1)}, bf16[8,52,64,128]{3,2,1,0:T(8,128)(2,1)}) fusion(bf16[2,8,52,64,128]{4,3,2,1,0:T(8,128)(2,1)} %get-tuple-element.304), kind=kLoop, calls=%fused_computation.9.clone.1 | loop fusion | bytes 27262976 | tf_op jit(solution)/shard_map/while/body/eval_jaxpr/squeeze | solution.py:74
  256.4 8.8 %gather_fusion = bf16[72,8,64,128]{3,2,1,0:T(8,128)(2,1)} fusion(bf16[8,52,64,128]{3,2,1,0:T(8,128)(2,1)} %get-tuple-element.263, s32[1024]{0:T(1024)S(1)} %pad_clamp_fusion.2), kind=kCustom, calls=%fused_computation.clone.clone.1 | custom fusion | bytes 18874656 | tf_op jit(solution)/shard_map/while/body/eval_jaxpr/gather | solution.py:73
  265.3 10.6 %copy.108 = bf16[8,8,9,64,128]{4,3,2,1,0:T(8,128)(2,1)} copy(bf16[8,8,9,64,128]{4,3,0,2,1:T(8,128)(2,1)} %bitcast.114) | data formatting | bytes 18874368 | tf_op jit(solution)/shard_map/while/body/eval_jaxpr/gather | solution.py:73
  275.9 9.1 %fusion.119 = (bf16[8,8,64,576]{3,2,1,0:T(8,128)(2,1)}, f32[8,8,64]{2,1,0:T(8,128)S(1)}) fusion(pred[8,64,576]{2,1,0:T(8,128)(4,1)S(1)} %broadcast_and_fusion.2, bf16[8,8,576,128]{3,2,1,0:T(8,128)(2,1)} %bitcast.115, bf16[8,24,64,128]{3,2,1,0:T(8,128)(2,1)} %get-tuple-element.303, s32[]{:T(128)S(6)} %select_n.223), kind=kOutput, calls=%fused_computation.118.clone.1 | convolution fusion | flops 618136128 | bytes 15876100 | tf_op jit(solution)/shard_map/while/body/eval_jaxpr/sub | solution.py:81
  285.0 8.8 %gather_fusion.1 = bf16[72,8,64,128]{3,2,1,0:T(8,128)(2,1)} fusion(bf16[8,52,64,128]{3,2,1,0:T(8,128)(2,1)} %get-tuple-element.265, s32[1024]{0:T(1024)S(1)} %pad_clamp_fusion.2), kind=kCustom, calls=%fused_computation.1.clone.clone.1 | custom fusion | bytes 18874656 | tf_op jit(solution)/shard_map/while/body/eval_jaxpr/gather | solution.py:74
  293.8 10.6 %copy.110 = bf16[72,8,64,128]{3,2,0,1:T(8,128)(2,1)} copy(bf16[72,8,64,128]{3,2,1,0:T(8,128)(2,1)} %gather_fusion.1) | data formatting | bytes 18874368 | tf_op jit(solution)/shard_map/while/body/eval_jaxpr/gather | solution.py:74
  304.4 8.8 %bitcast_convert_fusion.2 = bf16[8,64,2048]{2,1,0:T(8,128)(2,1)S(1)} fusion(bf16[8,128,2048,1]{2,1,0,3:T(8,128)(2,1)} %bitcast.123, f32[8,8,64]{2,0,1:T(8,128)S(1)} %copy.109, bf16[8,8,576,128]{3,2,1,0:T(8,128)(2,1)} %bitcast.116, bf16[8,8,64,576]{3,2,1,0:T(8,128)(2,1)} %get-tuple-element.266), kind=kOutput, calls=%fused_computation.16.clone.1 | convolution fusion | flops 2753560576 | bytes 20463616 | tf_op jit(solution)/shard_map/while/body/eval_jaxpr/hgqd,hde->gqe/dot_general | solution.py:87
  313.3 1.5 bitcast_dynamic-update-slice_fusion.2
  316.6 10.9 %slice_bitcast_fusion.3 = (bf16[8,52,64,128]{3,2,1,0:T(8,128)(2,1)}, bf16[8,52,64,128]{3,2,1,0:T(8,128)(2,1)}) fusion(bf16[2,8,52,64,128]{4,3,2,1,0:T(8,128)(2,1)} %get-tuple-element.304), kind=kLoop, calls=%fused_computation.9.clone.1 | loop fusion | bytes 27262976 | tf_op jit(solution)/shard_map/while/body/eval_jaxpr/squeeze | solution.py:74
  327.5 8.8 %gather_fusion = bf16[72,8,64,128]{3,2,1,0:T(8,128)(2,1)} fusion(bf16[8,52,64,128]{3,2,1,0:T(8,128)(2,1)} %get-tuple-element.263, s32[1024]{0:T(1024)S(1)} %pad_clamp_fusion.2), kind=kCustom, calls=%fused_computation.clone.clone.1 | custom fusion | bytes 18874656 | tf_op jit(solution)/shard_map/while/body/eval_jaxpr/gather | solution.py:73
  336.3 10.6 %copy.108 = bf16[8,8,9,64,128]{4,3,2,1,0:T(8,128)(2,1)} copy(bf16[8,8,9,64,128]{4,3,0,2,1:T(8,128)(2,1)} %bitcast.114) | data formatting | bytes 18874368 | tf_op jit(solution)/shard_map/while/body/eval_jaxpr/gather | solution.py:73
  346.9 9.1 %fusion.119 = (bf16[8,8,64,576]{3,2,1,0:T(8,128)(2,1)}, f32[8,8,64]{2,1,0:T(8,128)S(1)}) fusion(pred[8,64,576]{2,1,0:T(8,128)(4,1)S(1)} %broadcast_and_fusion.2, bf16[8,8,576,128]{3,2,1,0:T(8,128)(2,1)} %bitcast.115, bf16[8,24,64,128]{3,2,1,0:T(8,128)(2,1)} %get-tuple-element.303, s32[]{:T(128)S(6)} %select_n.223), kind=kOutput, calls=%fused_computation.118.clone.1 | convolution fusion | flops 618136128 | bytes 15876100 | tf_op jit(solution)/shard_map/while/body/eval_jaxpr/sub | solution.py:81
  356.1 8.8 %gather_fusion.1 = bf16[72,8,64,128]{3,2,1,0:T(8,128)(2,1)} fusion(bf16[8,52,64,128]{3,2,1,0:T(8,128)(2,1)} %get-tuple-element.265, s32[1024]{0:T(1024)S(1)} %pad_clamp_fusion.2), kind=kCustom, calls=%fused_computation.1.clone.clone.1 | custom fusion | bytes 18874656 | tf_op jit(solution)/shard_map/while/body/eval_jaxpr/gather | solution.py:74
  364.9 10.6 %copy.110 = bf16[72,8,64,128]{3,2,0,1:T(8,128)(2,1)} copy(bf16[72,8,64,128]{3,2,1,0:T(8,128)(2,1)} %gather_fusion.1) | data formatting | bytes 18874368 | tf_op jit(solution)/shard_map/while/body/eval_jaxpr/gather | solution.py:74
  375.5 8.8 %bitcast_convert_fusion.2 = bf16[8,64,2048]{2,1,0:T(8,128)(2,1)S(1)} fusion(bf16[8,128,2048,1]{2,1,0,3:T(8,128)(2,1)} %bitcast.123, f32[8,8,64]{2,0,1:T(8,128)S(1)} %copy.109, bf16[8,8,576,128]{3,2,1,0:T(8,128)(2,1)} %bitcast.116, bf16[8,8,64,576]{3,2,1,0:T(8,128)(2,1)} %get-tuple-element.266), kind=kOutput, calls=%fused_computation.16.clone.1 | convolution fusion | flops 2753560576 | bytes 20463616 | tf_op jit(solution)/shard_map/while/body/eval_jaxpr/hgqd,hde->gqe/dot_general | solution.py:87
  384.4 1.5 bitcast_dynamic-update-slice_fusion.2
  385.8 1.0 copy-done.1
  (84 shorter events, 6.5 us)
Async XLA Ops:
  0.0 13.9 %copy-start = (bf16[47,4096]{1,0:T(8,128)(2,1)S(1)}, bf16[47,4096]{1,0:T(8,128)(2,1)}, u32[]{:S(2)}) copy-start(bf16[47,4096]{1,0:T(8,128)(2,1)} %param.13) | copy-start | bytes 1155076
  0.0 42.1 %copy-start.5 = (bf16[64,2048]{1,0:T(8,128)(2,1)S(1)}, bf16[64,2048]{1,0:T(8,128)(2,1)}, u32[]{:S(2)}) copy-start(bf16[64,2048]{1,0:T(8,128)(2,1)} %param.18) | copy-start | bytes 786436
  2.4 21.1 %all-to-all-start = ((s32[64,1,1]{2,1,0:T(1,128)}), s32[64,1,1]{2,1,0:T(1,128)S(1)}, u32[]{:S(2)}, u32[]{:S(2)}) async-start(s32[64,1,1]{2,1,0:T(1,128)} %copy.55), calls=%async_computation | async-start | bytes 65536 | tf_op jit(solution)/shard_map/all_to_all | solution.py:129
  23.5 17.0 %all-to-all-start.1 = ((bf16[64,2,2048]{2,1,0:T(2,128)(2,1)}), bf16[64,2,2048]{2,1,0:T(2,128)(2,1)S(1)}, u32[]{:S(2)}, u32[]{:S(2)}) async-start(bf16[64,2,2048]{2,1,0:T(2,128)(2,1)} %reshape.260), calls=%async_computation.1 | async-start | bytes 1048576 | tf_op jit(solution)/shard_map/all_to_all | solution.py:122
  42.1 6.3 %copy-start.9 = (f32[2048]{0:T(1024)S(1)}, f32[2048]{0:T(1024)}, u32[]{:S(2)}) copy-start(f32[2048]{0:T(1024)} %param.19) | copy-start | bytes 24580
  56.7 10.1 %copy-start.4 = (bf16[1536,2048,1]{1,0,2:T(8,128)(2,1)S(1)}, bf16[1536,2048,1]{1,0,2:T(8,128)(2,1)}, u32[]{:S(2)}) copy-start(bf16[1536,2048,1]{1,0,2:T(8,128)(2,1)} %fusion.35) | copy-start | bytes 18874372
  56.7 10.2 %copy-start.11 = (bf16[2048,1024]{1,0:T(8,128)(2,1)S(1)}, bf16[2048,1024]{1,0:T(8,128)(2,1)}, u32[]{:S(2)}) copy-start(bf16[2048,1024]{1,0:T(8,128)(2,1)} %param.22) | copy-start | bytes 12582916
  74.0 3.9 %copy-start.2 = (bf16[1536,8,128]{2,0,1:T(8,128)(2,1)}, bf16[1536,8,128]{2,0,1:T(8,128)(2,1)S(1)}, u32[]{:S(2)}) copy-start(bf16[1536,8,128]{2,0,1:T(8,128)(2,1)S(1)} %fusion.52) | copy-start | bytes 9437188
  74.0 9.7 %copy-start.6 = (s32[24,8]{0,1:T(8,128)S(1)}, s32[24,8]{0,1:T(8,128)}, u32[]{:S(2)}) copy-start(s32[24,8]{0,1:T(8,128)} %param.16) | copy-start | bytes 2308
  74.0 9.7 %copy-start.10 = (s32[24,8]{0,1:T(8,128)S(1)}, s32[24,8]{0,1:T(8,128)}, u32[]{:S(2)}) copy-start(s32[24,8]{0,1:T(8,128)} %param.17) | copy-start | bytes 2308
  77.9 79.0 %collective-permute-start = (bf16[2,8,14,64,128]{4,3,2,1,0:T(8,128)(2,1)}, bf16[2,8,14,64,128]{4,3,2,1,0:T(8,128)(2,1)}, u32[]{:S(2)}, u32[]{:S(2)}) collective-permute-start(bf16[2,8,14,64,128]{4,3,2,1,0:T(8,128)(2,1)} %get-tuple-element.172), channel_id=1, source_target_pairs={{0,1},{1,2},{2,3},{3,4},{4,5},{5,6},{6,7},{7,8},{8,9},{9,10},{10,1... | collective-permute-start | bytes 11010056 | tf_op jit(solution)/shard_map/ppermute | solution.py:26
  82.2 80.7 %collective-permute-start.1 = (bf16[2,8,14,64,128]{4,3,2,1,0:T(8,128)(2,1)}, bf16[2,8,14,64,128]{4,3,2,1,0:T(8,128)(2,1)}, u32[]{:S(2)}, u32[]{:S(2)}) collective-permute-start(bf16[2,8,14,64,128]{4,3,2,1,0:T(8,128)(2,1)} %get-tuple-element.173), channel_id=1, source_target_pairs={{1,0},{2,1},{3,2},{4,3},{5,4},{6,5},{7,6},{8,7},{9,8},{10,9},{11,1... | collective-permute-start | bytes 11010056 | tf_op jit(solution)/shard_map/ppermute | solution.py:27
  84.3 78.6 %copy-start.3 = (bf16[1536,8,128]{2,0,1:T(8,128)(2,1)S(1)}, bf16[1536,8,128]{2,0,1:T(8,128)(2,1)}, u32[]{:S(2)}) copy-start(bf16[1536,8,128]{2,0,1:T(8,128)(2,1)} %copy-done.2) | copy-start | bytes 9437188
  172.6 1.8 copy-start.7
  233.4 10.3 %copy-start.8 = (s32[64]{0:T(128)S(1)}, s32[64]{0:T(128)}, u32[]{:S(2)}) copy-start(s32[64]{0:T(128)} %copy-done.7) | copy-start | bytes 772 | tf_op jit(solution)/shard_map/while
  243.7 1.8 copy-start.7
  304.4 10.3 %copy-start.8 = (s32[64]{0:T(128)S(1)}, s32[64]{0:T(128)}, u32[]{:S(2)}) copy-start(s32[64]{0:T(128)} %copy-done.7) | copy-start | bytes 772 | tf_op jit(solution)/shard_map/while
  314.7 1.8 copy-start.7
  375.5 10.3 %copy-start.8 = (s32[64]{0:T(128)S(1)}, s32[64]{0:T(128)}, u32[]{:S(2)}) copy-start(s32[64]{0:T(128)} %copy-done.7) | copy-start | bytes 772 | tf_op jit(solution)/shard_map/while
  385.8 1.0 copy-start.1
where the time goes:
time: 388 us; the launch traced here: 387 us
  local copies, waits for them, and re-layouts  161 us (41%)
  matrix products  89.9 us (23%)
  waiting for transfers between devices  84.3 us (22%)
  other arithmetic  26.6 us (7%)
  starting transfers between devices  22.4 us (6%)
    ppermute x1, waiting for transfers between devices, with_halo(): before = lax.ppermute(last, axis, up)  61.3 us
    gather x6, local copies, waits for them, and re-layouts, attend_block(): extended[0][:, index_block]  58.3 us
    gather x6, local copies, waits for them, and re-layouts, attend_block(): extended[1][:, index_block]  58.3 us
    squeeze x3, local copies, waits for them, and re-layouts, attend_block(): extended[1][:, index_block]  32.6 us
    dot_general x3, matrix products, head_major(): jnp.einsum('nc,chd->hnd', normed, shaped, preferred_element_type=jnp.floa...  28.6 us
    sub x3, matrix products, attend_block(): raised = jnp.where(allowed, jnp.exp(scores - row_max), 0.0)  27.4 us
    dot_general x3, matrix products, attend_block(): jnp.einsum('hgqd,hde->gqe', attended, out_heads, preferred_element_type=j...  26.5 us
    all_to_all x1, starting transfers between devices, local(): lax.all_to_all(places.reshape(devices, capacity), 'tile', split_axis=0, c...  11.5 us
  transfers between devices with their start and end apart: 4, of which 4 were waited for; matrix products, arithmetic and copies ran while one was open for 4% of the time, Pallas kernels for 0%

commit v1 on v0

v1 whole, which is shorter than its diff:
```python
import math

import jax
import jax.numpy as jnp
import numpy as np
from jax import lax
from jax.experimental import pallas as pl
from jax.experimental.pallas import tpu as pltpu
from jax.sharding import PartitionSpec as P

D = 2048
HEADS = 8
HEAD = 128
LAT = 64
SIDE = 8
RADIUS = 6
HALO = 14
TILES = 24
EXT = TILES + 2 * HALO
EPSILON = 1e-06
AWAY = -1e38
GROUP = 4
SCALE = HEAD ** -0.5 * math.log2(math.e)

BF = jnp.bfloat16
F32 = jnp.float32


def place_constants():
    spread = np.zeros((GROUP, 2, 8, 8, GROUP, 8, 4), np.float32)
    for t in range(GROUP):
        for form in range(2):
            for r in range(8):
                for s in range(8):
                    spread[t, form, r, s, t, r, (s + 1 + 2 * form) % 4] = 1
    spread = spread.reshape(GROUP * 128, GROUP * 32)
    order = np.zeros((GROUP, 2, 2, 2, 4, 2, GROUP, 8, 4), np.float32)
    back = np.zeros((GROUP, 8, 8, GROUP, 2, 2, 2, 4, 2), np.float32)
    for t in range(GROUP):
        for a in range(2):
            for b in range(2):
                for p in range(2):
                    for r in range(4):
                        for c in range(2):
                            order[t, a, b, p, r, c, t, 4 * a + r, 2 * b + c] = 1
                            back[t, 4 * a + r, 4 * b + 2 * c + p, t, a, b, p, r, c] = 1
    order = order.reshape(GROUP * 64, GROUP * 32)
    back = back.reshape(GROUP * 64, GROUP * 64)
    query_extra = np.zeros((HEADS, 2, 4, 2, 128), np.float32)
    for p in range(2):
        for r in range(4):
            for c in range(2):
                query_extra[:, p, r, c, 8 + r] = 1
                query_extra[:, p, r, c, 12 + 2 * c + p] = 1
    query_extra = query_extra.reshape(HEADS * 16, 128)
    key_extra = np.zeros((2, 2, 2, 16, 8, 128), np.float32)
    for a in range(2):
        for b in range(2):
            for p in range(2):
                for row in range(16):
                    for s in range(8):
                        col = 2 * s + p
                        tile_row = (4 * a - 6 + row) // 8 + 1
                        tile_col = (4 * b - 6 + col) // 8 + 1
                        region = tile_row * 3 + tile_col
                        lane = key_extra[a, b, p, row, s]
                        if region != 4:
                            lane[region - (region > 4)] = 1
                        for i in range(4):
                            lane[8 + i] = 0 if i <= row <= i + 2 * RADIUS else AWAY
                            lane[12 + i] = 0 if i <= col <= i + 2 * RADIUS else AWAY
    key_extra = key_extra.reshape(4, 256, 128)
    as_bf = lambda x: np.asarray(x, np.float32).astype(jnp.bfloat16)
    return tuple(as_bf(x) for x in (spread, order, back, query_extra, key_extra))


def split(x):
    high = x.astype(BF)
    low = (x - high.astype(F32)).astype(BF)
    return high, low


def dot(a, b):
    return jnp.dot(a, b, preferred_element_type=F32)


def dot_t(a, b):
    return lax.dot_general(a, b, (((1,), (1,)), ((), ())), preferred_element_type=F32)


def attend_kernel(
    owner_ref, slot_ref, ext_ref, mix_ref, out_mix_ref, spread_ref, order_ref, back_ref,
    query_extra_ref, key_extra_ref, out_ref, z_ref, q_ref, u_ref,
):
    step = pl.program_id(0)
    me = lax.axis_index("tile")
    low_lane = lax.broadcasted_iota(jnp.int32, (16, 128), 1) < LAT

    @pl.when(step == 0)
    def _():
        rows = GROUP * 32
        spread = spread_ref[...]
        groups = EXT // GROUP
        for g in range(0, groups, 2):
            pair = [ext_ref[pl.ds(k * rows, rows), :] for k in range(g, min(g + 2, groups))]
            made = dot(spread, jnp.concatenate(pair, axis=1)).astype(BF)
            for k in range(len(pair)):
                z_ref[pl.ds((g + k) * GROUP * 128, GROUP * 128), :] = made[:, k * 128 : k * 128 + 128]
        order = order_ref[...]
        parity = (lax.broadcasted_iota(jnp.int32, (GROUP * 64, 128), 0) // 8) % 2
        half = lax.broadcasted_iota(jnp.int32, (GROUP * 64, 128), 1) // LAT
        keep = (parity == half).astype(F32)
        for g in range(TILES // GROUP):
            own = ext_ref[pl.ds(HALO * 32 + g * rows, rows), :]
            picked = (dot(order, own) * keep).astype(BF)
            both = jnp.concatenate([picked, picked], axis=1)
            q_ref[pl.ds(g * GROUP * 64, GROUP * 64), :] = dot(both, mix_ref[...]).astype(BF)

    sub = lax.broadcasted_iota(jnp.int32, (16, 128), 0) % 8
    lane_row = lax.broadcasted_iota(jnp.int32, (128, 128), 1)
    ones = jnp.ones((256, 128), BF)
    for t in range(GROUP):
        tile = step * GROUP + t
        places = []
        extra = query_extra_ref[...].astype(F32)
        for n in range(8):
            owner = owner_ref[tile, n]
            place = HALO + (owner - me) * TILES + slot_ref[tile, n]
            places.append(jnp.where(owner >= 0, place, HALO + tile))
            bias = jnp.where(owner >= 0, 0.0, AWAY).astype(F32)
            extra = jnp.where(lane_row == n, bias, extra)
        extra = extra.astype(BF)
        places = places[:4] + [HALO + tile] + places[4:]
        bases = [p * 128 for p in places]
        for b in range(2):
            strips = []
            for tile_row, pairs in ((0, (1, 2, 3)), (1, (0, 1, 2, 3)), (2, (0, 1, 2))):
                for pair in pairs:
                    left, mid, right = (
                        z_ref[pl.ds(pl.multiple_of(bases[tile_row * 3 + k] + b * 64 + pair * 16, 16), 16), :]
                        for k in range(3)
                    )
                    first, last = ((3, 7), (1, 5))[b]
                    strips.append(jnp.where(sub < first, left, jnp.where(sub < last, mid, right)))
            zero = jnp.zeros((16, 128), BF)
            even = [jnp.where(low_lane, s, zero) for s in strips]
            odd = [jnp.where(low_lane, zero, s) for s in strips]
            for a in range(2):
                quad = 2 * a + b
                cut = slice(2 * a, 2 * a + 8)
                held = jnp.concatenate(even[cut] + odd[cut], axis=0)
                keys = jnp.concatenate([held, key_extra_ref[quad]], axis=1)
                values = jnp.concatenate([held, ones], axis=1)
                block = q_ref[pl.ds(pl.multiple_of(tile * 64 + quad * 16, 16), 16), :]
                query = jnp.concatenate([block[:, h * 128 : h * 128 + 128] for h in range(HEADS)], axis=0)
                scores = dot_t(jnp.concatenate([query, extra], axis=1), keys)
                raised = jnp.exp2(scores - jnp.max(scores, axis=1, keepdims=True)).astype(BF)
                summed = dot(raised, values)
                part = summed[:, :128]
                part = (part + pltpu.roll(part, LAT, 1)) / summed[:, 128:]
                joined = [
                    jnp.where(low_lane, part[32 * k : 32 * k + 16], part[32 * k + 16 : 32 * k + 32])
                    for k in range(HEADS // 2)
                ]
                u_ref[pl.ds(t * 64 + quad * 16, 16), :] = jnp.concatenate(joined, axis=1).astype(BF)
    placed = dot(back_ref[...], u_ref[...]).astype(BF)
    for n in range(0, D, 512):
        out_ref[:, n : n + 512] = dot(placed, out_mix_ref[:, n : n + 512]).astype(BF)


def attend(owner, slot, ext, mix, out_mix):
    constants = place_constants()
    smem = pl.BlockSpec(memory_space=pltpu.SMEM)
    vmem = pl.BlockSpec(memory_space=pltpu.VMEM)
    rows = GROUP * 64
    return pl.pallas_call(
        attend_kernel,
        grid=(TILES // GROUP,),
        out_shape=jax.ShapeDtypeStruct((TILES * 64, D), BF),
        in_specs=[smem, smem] + [vmem] * 8,
        out_specs=pl.BlockSpec((rows, D), lambda i: (i, 0)),
        scratch_shapes=[
            pltpu.VMEM((EXT * 128, 128), BF),
            pltpu.VMEM((TILES * 64, HEADS * 128), BF),
            pltpu.VMEM((rows, HEADS * LAT), BF),
        ],
        compiler_params=pltpu.CompilerParams(vmem_limit_bytes=48 * 2**20),
        cost_estimate=pl.CostEstimate(flops=8 * 10**9, bytes_accessed=10**7, transcendentals=3 * 10**6),
        name="attend",
    )(owner, slot, ext, mix, out_mix, *[jnp.asarray(c) for c in constants])


CHUNK = 512


def fold_kernel(
    embed_ref, gain_ref, wq_ref, wk_ref, wv_ref, wo_ref, mix_ref, out_mix_ref,
    wq, wk, wv, wo, sems,
):
    copies = []
    for w, (source, target) in enumerate(((wq_ref, wq), (wk_ref, wk), (wv_ref, wv), (wo_ref, wo))):
        row_count = source.shape[0] // 4
        for c in range(4):
            cut = pl.ds(c * row_count, row_count)
            copy = pltpu.make_async_copy(source.at[cut], target.at[cut], sems.at[w, c])
            copy.start()
            copies.append(copy)
    scaled = embed_ref[...].astype(F32) * gain_ref[...]
    stacked = jnp.concatenate(split(scaled), axis=0)

    def folded(w, held):
        total = jnp.zeros((2 * LAT, HEADS * HEAD), F32)
        for c in range(4):
            copies[w * 4 + c].wait()
            total += dot(stacked[:, c * CHUNK : (c + 1) * CHUNK], held[pl.ds(c * CHUNK, CHUNK), :])
        return split(total[:LAT] + total[LAT:])

    query_high, query_low = folded(0, wq)
    key_high, key_low = folded(1, wk)
    for h in range(HEADS):
        cut = slice(h * HEAD, (h + 1) * HEAD)
        left = jnp.concatenate([query_high[:, cut], query_low[:, cut], query_high[:, cut]], axis=1)
        right = jnp.concatenate([key_high[:, cut], key_high[:, cut], key_low[:, cut]], axis=1)
        high, low = split(dot_t(left, jnp.concatenate([right, right], axis=0)) * SCALE)
        mix_ref[:, cut] = jnp.concatenate([high, high, low, low], axis=0)
    value = jnp.concatenate(folded(2, wv), axis=0)
    for h in range(HEADS):
        cut = slice(h * HEAD, (h + 1) * HEAD)
        if h % 2 == 0:
            copies[12 + h // 2].wait()
        for n in range(0, D, 512):
            made = dot(value[:, cut], wo[cut, n : n + 512])
            out_mix_ref[pl.ds(h * LAT, LAT), n : n + 512] = (made[:LAT] + made[LAT:]).astype(BF)


def fold(w_embed, norm_gain, w_query, w_key, w_value, w_out):
    vmem = pl.BlockSpec(memory_space=pltpu.VMEM)
    hbm = pl.BlockSpec(memory_space=pl.ANY)
    return pl.pallas_call(
        fold_kernel,
        out_shape=(
            jax.ShapeDtypeStruct((4 * LAT, HEADS * HEAD), BF),
            jax.ShapeDtypeStruct((HEADS * LAT, D), BF),
        ),
        in_specs=[vmem, vmem, hbm, hbm, hbm, hbm],
        out_specs=(vmem, vmem),
        scratch_shapes=[
            pltpu.VMEM(w.shape, BF) for w in (w_query, w_key, w_value, w_out)
        ] + [pltpu.SemaphoreType.DMA((4, 4))],
        compiler_params=pltpu.CompilerParams(vmem_limit_bytes=48 * 2**20),
        cost_estimate=pl.CostEstimate(flops=3 * 10**9, bytes_accessed=2 * 10**7, transcendentals=0),
        name="fold",
    )(w_embed, norm_gain.reshape(1, D), w_query, w_key, w_value, w_out)


def local(
    tile_latents, tile_owner, tile_position, neighbour_owner, neighbour_slot,
    w_embed, norm_gain, w_query, w_key, w_value, w_out,
):
    devices = lax.axis_size("tile")
    mix, out_mix = fold(w_embed, norm_gain, w_query, w_key, w_value, w_out)
    chosen = jnp.arange(devices)[:, None] == tile_owner[None, :]
    outgoing = dot(chosen.astype(BF), tile_latents)
    dead = ~jnp.any(chosen, axis=1, keepdims=True)
    outgoing = jnp.where(dead, 512.0, outgoing).astype(BF)
    arrived = lax.all_to_all(outgoing, "tile", split_axis=0, concat_axis=0, tiled=True)
    live = arrived[:, 0] < 100.0
    rank = jnp.cumsum(live.astype(jnp.int32)) - 1
    taken = (jnp.arange(TILES)[:, None] == rank[None, :]) & live[None, :]
    owned = dot(taken.astype(BF), arrived).reshape(TILES * 64, LAT)
    gram = dot_t(w_embed, w_embed) / D
    mean = jnp.sum(jnp.dot(owned, gram, precision=lax.Precision.HIGHEST) * owned, axis=1, keepdims=True)
    scaled = (owned * lax.rsqrt(jnp.maximum(mean, 0.0) + EPSILON)).astype(BF).reshape(TILES * 32, 128)
    up = [(i, (i + 1) % devices) for i in range(devices)]
    down = [(j, i) for i, j in up]
    before = lax.ppermute(scaled[(TILES - HALO) * 32 :], "tile", up)
    after = lax.ppermute(scaled[: HALO * 32], "tile", down)
    ext = jnp.concatenate([before, scaled, after], axis=0)
    return attend(neighbour_owner, neighbour_slot, ext, mix, out_mix)


def solution(mesh):
    both = P(("dp", "tile"), None)
    flat = P(("dp", "tile"))
    return jax.shard_map(
        local,
        mesh=mesh,
        in_specs=(both, flat, flat, both, both, P(), P(), P(), P(), P(), P()),
        out_specs=both,
        check_vma=False,
    )
```

time: 388 us -> 108 us (0.28)
  local copies, waits for them, and re-layouts: 161 us -> 25.7 us
  matrix products: 89.9 us -> 6.54 us
  waiting for transfers between devices: 84.3 us -> 8.48 us
  Pallas kernels: 0 us -> 43.6 us
  other arithmetic: 26.6 us -> 6.44 us
  starting transfers between devices: 22.4 us -> 16.1 us
    gather x12 -> x0, local copies, waits for them, and re-layouts: 117 us -> none  [the longest x6 58.3 us: attend_block(): extended[0][:, index_block]]
    ppermute x2, waiting for transfers between devices: 67.2 us -> 5.53 us  [the longest x1 5.53 us: local(): before = lax.ppermute(scaled[(TILES - HALO) * 32:], 'tile', up)]
    dot_general x9 -> x4, matrix products: 62.5 us -> 6.54 us  [the longest x1 2.32 us: local(): jnp.dot(owned, gram, precision=lax.Precision.HIGHEST) * owned]
    pallas_call x0 -> x2, Pallas kernels: none -> 43.6 us  [the longest x1 36.7 us: attend(): pl.pallas_call(attend_kernel, grid=(TILES // GROUP,), out_shape=jax.Shape...]
    squeeze x6 -> x0, local copies, waits for them, and re-layouts: 32.6 us -> none  [the longest x3 32.6 us: attend_block(): extended[1][:, index_block]]
    sub x3 -> x0, matrix products: 27.4 us -> none  [attend_block(): raised = jnp.where(allowed, jnp.exp(scores - row_max), 0.0)]
    all_to_all x2 -> x1, waiting for transfers between devices: 17.1 us -> 2.95 us  [local(): lax.all_to_all(outgoing, 'tile', split_axis=0, concat_axis=0, tiled=True)]
    concatenate x3 -> x1, other arithmetic: 9.84 us -> 0.98 us  [local(): ext = jnp.concatenate([before, scaled, after], axis=0)]
  transfers between devices with their start and end apart: 4 -> 3, of which waited for: 4 -> 2; matrix products, arithmetic and copies ran while one was open for 4% -> 8% of each run, Pallas kernels for 0% -> 6%
where the time goes in v1:
time: 108 us; the launch traced here: 107 us
  Pallas kernels  43.6 us (40%)
  local copies, waits for them, and re-layouts  25.7 us (24%)
  starting transfers between devices  16.1 us (15%)
  waiting for transfers between devices  8.48 us (8%)
  matrix products  6.54 us (6%)
  other arithmetic  6.44 us (6%)
    pallas_call x1, Pallas kernels, attend(): pl.pallas_call(attend_kernel, grid=(TILES // GROUP,), out_shape=jax.Shape...  36.7 us
    all_to_all x1, starting transfers between devices, local(): lax.all_to_all(outgoing, 'tile', split_axis=0, concat_axis=0, tiled=True)  11.8 us
    unnamed x23, local copies, waits for them, and re-layouts  10.8 us
    pallas_call x1, Pallas kernels, fold(): pl.pallas_call(fold_kernel, out_shape=(jax.ShapeDtypeStruct((4 * LAT, HEA...  6.9 us
    ppermute x1, waiting for transfers between devices, local(): before = lax.ppermute(scaled[(TILES - HALO) * 32:], 'tile', up)  5.53 us
    ppermute x1, starting transfers between devices, local(): after = lax.ppermute(scaled[:HALO * 32], 'tile', down)  4.31 us
    reshape x3, local copies, waits for them, and re-layouts, local(): owned = dot(taken.astype(BF), arrived).reshape(TILES * 64, LAT)  4.13 us
    slice x2, local copies, waits for them, and re-layouts, local(): before = lax.ppermute(scaled[(TILES - HALO) * 32:], 'tile', up)  3.58 us
  transfers between devices with their start and end apart: 3, of which 2 were waited for; matrix products, arithmetic and copies ran while one was open for 8% of the time, Pallas kernels for 6%

profile of v1, /device:TPU:0, one launch (start us, length us, event | category | flops | bytes accessed | tf_op | source)
XLA Modules:
  0.0 107.0 jit_solution(11215698032859406161)
XLA Ops:
  0.0 0.0 copy-start
  0.0 0.8 fusion.3
  0.8 0.2 copy-done
  1.0 1.1 fusion.1
  2.1 0.5 broadcast.39
  2.6 1.0 reduce.4
  3.6 1.2 %reshape.70 = bf16[64,2,2048]{2,1,0:T(2,128)(2,1)} reshape(bf16[64,4096]{1,0:T(8,128)(2,1)S(1)} %reduce.4) | data formatting | bytes 1048576
  4.8 11.8 %all-to-all-start = ((bf16[64,2,2048]{2,1,0:T(2,128)(2,1)}), bf16[64,2,2048]{2,1,0:T(2,128)(2,1)}, u32[]{:S(2)}, u32[]{:S(2)}) async-start(bf16[64,2,2048]{2,1,0:T(2,128)(2,1)} %reshape.70), calls=%async_computation | async-start | bytes 1048576 | tf_op jit(solution)/shard_map/all_to_all | solution.py:266
  16.5 0.8 copy.40.owner_ref
  17.3 0.8 copy.41.slot_ref
  18.1 1.9 %convolution_multiply_fusion.1 = f32[64,64]{1,0:T(8,128)} fusion(bf16[64,2048]{1,0:T(8,128)(2,1)} %embed_ref.1), kind=kOutput, calls=%fused_computation.5 | convolution fusion | flops 16781312 | bytes 278528 | tf_op jit(solution)/shard_map/dot_general | solution.py:88
  20.0 0.0 copy-done.1
  20.0 0.0 copy-done.2
  20.0 6.9 %fold.1 = (bf16[256,1024]{1,0:T(8,128)(2,1)S(1)}, bf16[512,2048]{1,0:T(8,128)(2,1)S(1)}) custom-call(bf16[64,2048]{1,0:T(8,128)(2,1)S(1)} %copy-done.1, f32[1,2048]{1,0:T(1,128)S(1)} %bitcast.13, bf16[2048,1024]{1,0:T(8,128)(2,1)} %wq_ref.1, bf16[2048,1024]{1,0:T(8,128)(2,1)} %wk_ref.1, bf16[2048,1024]{1,0:T(8,128)(2,1)} %wv_ref.1, bf16[1024,2048]{1,0:T(8,128)(2,1)} %wo_ref.1), custom_call_target="tpu_custom_call" | custom-call | flops 3000000000 | bytes 20000000 | tf_op jit(solution)/shard_map/fold/pallas_call | solution.py:239
  26.9 3.0 %all-to-all-done = bf16[64,2,2048]{2,1,0:T(2,128)(2,1)} async-done(((bf16[64,2,2048]{2,1,0:T(2,128)(2,1)}), bf16[64,2,2048]{2,1,0:T(2,128)(2,1)}, u32[]{:S(2)}, u32[]{:S(2)}) %all-to-all-start) | async-done | bytes 524320 | tf_op jit(solution)/shard_map/all_to_all | solution.py:266
  29.8 4.4 %reshape.71 = bf16[64,1,4096]{2,1,0:T(2,128)(2,1)} reshape(bf16[64,2,2048]{2,1,0:T(2,128)(2,1)} %all-to-all-done) | data formatting | bytes 1048576
  34.3 1.8 %copy.44 = bf16[64,1,4096]{2,0,1:T(8,128)(2,1)S(1)} copy(bf16[64,1,4096]{2,1,0:T(2,128)(2,1)} %reshape.71) | data formatting | bytes 1048576
  36.1 0.0 copy-start.8
  36.1 0.8 copy-done.8
  36.9 0.1 fusion.10
  37.0 0.1 reduce-window.8
  37.1 0.1 add_reduce_fusion
  37.2 1.2 %fusion.6 = f32[24,4096]{1,0:T(8,128)S(1)} fusion(bf16[64,4096]{1,0:T(8,128)(2,1)} %bitcast.15, s32[64]{0:T(128)S(1)} %add_reduce_fusion, pred[64]{0:T(512)(128)(4,1)S(1)} %get-tuple-element.9), kind=kOutput, calls=%fused_computation.17 | convolution fusion | flops 12585984 | bytes 917824 | tf_op jit(solution)/shard_map/dot_general | solution.py:84
  38.5 0.8 reshape.66
  39.3 1.2 %reshape.65 = f32[1536,64]{1,0:T(8,128)} reshape(f32[24,4096]{1,0:T(8,128)S(1)} %fusion.6) | data formatting | bytes 786432 | tf_op jit(solution)/shard_map/reshape | solution.py:270
  40.5 2.1 %copy.37 = f32[1536,64]{0,1:T(8,128)} copy(f32[1536,64]{1,0:T(8,128)} %reshape.65) | data formatting | bytes 786432 | tf_op jit(solution)/shard_map/reshape | solution.py:270
  42.6 2.3 %fusion.2 = f32[1536]{0:T(1024)S(1)} fusion(f32[1536,64]{0,1:T(8,128)} %copy.37, f32[1536,64]{1,0:T(8,128)} %reshape.65, f32[64,64]{1,0:T(8,128)} %convolution_multiply_fusion.1), kind=kOutput, calls=%fused_computation.4 | convolution fusion | flops 75692544 | bytes 808960 | tf_op jit(solution)/shard_map/dot_general | solution.py:272
  44.9 2.2 %multiply_convert_fusion = bf16[1536,64]{1,0:T(8,128)(2,1)} fusion(f32[1536,64]{1,0:T(8,128)} %reshape.65, f32[1536]{0:T(1024)S(1)} %add_rsqrt_fusion), kind=kLoop, calls=%fused_computation.6 | loop fusion | flops 196608 | bytes 595968 | tf_op jit(solution)/shard_map/convert_element_type | solution.py:273
  47.1 1.1 %rsqrt.13 = f32[768,2]{1,0:T(8,128)} reshape(f32[1536]{0:T(1024)S(1)} %add_rsqrt_fusion) | data formatting | bytes 12288 | tf_op jit(solution)/shard_map/rsqrt | solution.py:273
  48.2 1.8 %fusion.12 = (bf16[896,64]{1,0:T(8,128)(2,1)}, bf16[896,64]{1,0:T(8,128)(2,1)}) fusion(bf16[1536,64]{1,0:T(8,128)(2,1)} %multiply_convert_fusion), kind=kLoop, calls=%fused_computation.23 | loop fusion | bytes 458752 | tf_op jit(solution)/shard_map/slice | solution.py:276
  50.0 1.7 %slice.17 = bf16[448,128]{1,0:T(8,128)(2,1)} reshape(bf16[896,64]{1,0:T(8,128)(2,1)} %get-tuple-element.11) | data formatting | bytes 229376 | tf_op jit(solution)/shard_map/slice | solution.py:276
  51.8 1.8 %slice.19 = bf16[448,128]{1,0:T(8,128)(2,1)} reshape(bf16[896,64]{1,0:T(8,128)(2,1)} %get-tuple-element.12) | data formatting | bytes 229376 | tf_op jit(solution)/shard_map/slice | solution.py:277
  53.5 4.3 %collective-permute-start.1 = (bf16[448,128]{1,0:T(8,128)(2,1)}, bf16[448,128]{1,0:T(8,128)(2,1)}, u32[]{:S(2)}, u32[]{:S(2)}) collective-permute-start(bf16[448,128]{1,0:T(8,128)(2,1)} %slice.19), channel_id=1, source_target_pairs={{1,0},{2,1},{3,2},{4,3},{5,4},{6,5},{7,6},{8,7},{9,8},{10,9},{11,1... | collective-permute-start | bytes 344072 | tf_op jit(solution)/shard_map/ppermute | solution.py:277
  57.8 0.0 collective-permute-start
  57.8 1.1 %copy.38 = f32[768,2]{0,1:T(2,128)S(1)} copy(f32[768,2]{1,0:T(8,128)} %rsqrt.13) | data formatting | bytes 12288 | tf_op jit(solution)/shard_map/rsqrt | solution.py:273
  59.0 0.8 mul.21
  59.8 1.9 %copy.39 = f32[768,128]{1,0:T(8,128)} copy(f32[768,128]{0,1:T(8,128)} %bitcast.16) | data formatting | bytes 786432 | tf_op jit(solution)/shard_map/mul | solution.py:273
  61.7 1.2 %multiply_convert_fusion.1 = bf16[768,128]{1,0:T(8,128)(2,1)S(1)} fusion(f32[768,128]{1,0:T(8,128)} %reshape.66, f32[768,128]{1,0:T(8,128)} %copy.39), kind=kLoop, calls=%fused_computation.9 | loop fusion | flops 196608 | bytes 983040 | tf_op jit(solution)/shard_map/convert_element_type | solution.py:273
  62.8 0.0 collective-permute-done.1
  62.8 5.5 %collective-permute-done = bf16[448,128]{1,0:T(8,128)(2,1)} collective-permute-done((bf16[448,128]{1,0:T(8,128)(2,1)}, bf16[448,128]{1,0:T(8,128)(2,1)}, u32[]{:S(2)}, u32[]{:S(2)}) %collective-permute-start) | collective-permute-done | bytes 114720 | tf_op jit(solution)/shard_map/ppermute | solution.py:276
  68.4 1.0 pad_maximum_fusion.ext_ref
  69.4 0.0 copy-done.3
  69.4 0.0 copy-done.4
  69.4 0.0 copy-done.6
  69.4 0.0 copy-done.7
  69.4 0.0 copy-start.5
  69.4 0.9 copy-done.5
  70.3 36.7 %attend.1 = bf16[1536,2048]{1,0:T(8,128)(2,1)} custom-call(s32[24,8]{1,0:T(8,128)S(1)} %copy.40.owner_ref, s32[24,8]{1,0:T(8,128)S(1)} %copy.41.slot_ref, bf16[1664,128]{1,0:T(8,128)(2,1)S(1)} %pad_maximum_fusion.ext_ref, bf16[256,1024]{1,0:T(8,128)(2,1)S(1)} %get-tuple-element.7.mix_ref, bf16[512,2048]{1,0:T(8,128)(2,1)S(1)} %get-tuple-element.8.out_mix_ref, ...), custom_call_target="tpu_custom_call" | custom-call | flops 8000000000 | bytes 10000000 | tf_op jit(solution)/shard_map/attend/pallas_call | solution.py:176
  (8 shorter events, 0.0 us)
Async XLA Ops:
  0.0 1.0 copy-start
  0.0 20.0 %copy-start.1 = (bf16[64,2048]{1,0:T(8,128)(2,1)S(1)}, bf16[64,2048]{1,0:T(8,128)(2,1)}, u32[]{:S(2)}) copy-start(bf16[64,2048]{1,0:T(8,128)(2,1)} %embed_ref.1) | copy-start | bytes 786436
  0.0 20.0 %copy-start.2 = (f32[2048]{0:T(1024)S(1)}, f32[2048]{0:T(1024)}, u32[]{:S(2)}) copy-start(f32[2048]{0:T(1024)} %param.21) | copy-start | bytes 24580
  4.8 25.1 %all-to-all-start = ((bf16[64,2,2048]{2,1,0:T(2,128)(2,1)}), bf16[64,2,2048]{2,1,0:T(2,128)(2,1)}, u32[]{:S(2)}, u32[]{:S(2)}) async-start(bf16[64,2,2048]{2,1,0:T(2,128)(2,1)} %reshape.70), calls=%async_computation | async-start | bytes 1048576 | tf_op jit(solution)/shard_map/all_to_all | solution.py:266
  36.1 0.8 copy-start.8
  42.6 26.8 %copy-start.3 = (bf16[4,256,128]{2,1,0:T(8,128)(2,1)S(1)}, bf16[4,256,128]{2,1,0:T(8,128)(2,1)}, u32[]{:S(2)}) copy-start(bf16[4,256,128]{2,1,0:T(8,128)(2,1)} %constant.35.clone.key_extra_ref) | copy-start | bytes 786436
  42.6 26.8 %copy-start.4 = (bf16[256,256]{1,0:T(8,128)(2,1)S(1)}, bf16[256,256]{1,0:T(8,128)(2,1)}, u32[]{:S(2)}) copy-start(bf16[256,256]{1,0:T(8,128)(2,1)} %constant.33.clone.back_ref) | copy-start | bytes 393220
  42.6 26.8 %copy-start.6 = (bf16[256,128]{1,0:T(8,128)(2,1)S(1)}, bf16[256,128]{1,0:T(8,128)(2,1)}, u32[]{:S(2)}) copy-start(bf16[256,128]{1,0:T(8,128)(2,1)} %constant.32.clone.order_ref) | copy-start | bytes 196612
  42.6 26.8 %copy-start.7 = (bf16[128,128]{1,0:T(8,128)(2,1)S(1)}, bf16[128,128]{1,0:T(8,128)(2,1)}, u32[]{:S(2)}) copy-start(bf16[128,128]{1,0:T(8,128)(2,1)} %constant.34.clone.query_extra_ref) | copy-start | bytes 98308
  53.5 9.3 %collective-permute-start.1 = (bf16[448,128]{1,0:T(8,128)(2,1)}, bf16[448,128]{1,0:T(8,128)(2,1)}, u32[]{:S(2)}, u32[]{:S(2)}) collective-permute-start(bf16[448,128]{1,0:T(8,128)(2,1)} %slice.19), channel_id=1, source_target_pairs={{1,0},{2,1},{3,2},{4,3},{5,4},{6,5},{7,6},{8,7},{9,8},{10,9},{11,1... | collective-permute-start | bytes 344072 | tf_op jit(solution)/shard_map/ppermute | solution.py:277
  57.8 10.5 %collective-permute-start = (bf16[448,128]{1,0:T(8,128)(2,1)}, bf16[448,128]{1,0:T(8,128)(2,1)}, u32[]{:S(2)}, u32[]{:S(2)}) collective-permute-start(bf16[448,128]{1,0:T(8,128)(2,1)} %slice.17), channel_id=1, source_target_pairs={{0,1},{1,2},{2,3},{3,4},{4,5},{5,6},{6,7},{7,8},{8,9},{9,10},{10,1... | collective-permute-start | bytes 344072 | tf_op jit(solution)/shard_map/ppermute | solution.py:276
  69.4 0.9 copy-start.5

commit v2 on v1

--- a/solution.py
+++ b/solution.py
@@ -16,6 +16,7 @@
 RADIUS = 6
 HALO = 14
 TILES = 24
+TILE_VALUES = 4096
 EXT = TILES + 2 * HALO
 EPSILON = 1e-06
 AWAY = -1e38
@@ -88,6 +89,9 @@
     return lax.dot_general(a, b, (((1,), (1,)), ((), ())), preferred_element_type=F32)
 
 
+LAG1, LAG2, LAG3 = 2, 4, 6
+
+
 def attend_kernel(
     owner_ref, slot_ref, ext_ref, mix_ref, out_mix_ref, spread_ref, order_ref, back_ref,
     query_extra_ref, key_extra_ref, out_ref, z_ref, q_ref, u_ref,
@@ -119,7 +123,9 @@
     sub = lax.broadcasted_iota(jnp.int32, (16, 128), 0) % 8
     lane_row = lax.broadcasted_iota(jnp.int32, (128, 128), 1)
     ones = jnp.ones((256, 128), BF)
-    for t in range(GROUP):
+    zero = jnp.zeros((16, 128), BF)
+
+    def region(t):
         tile = step * GROUP + t
         places = []
         extra = query_extra_ref[...].astype(F32)
@@ -129,40 +135,71 @@
             places.append(jnp.where(owner >= 0, place, HALO + tile))
             bias = jnp.where(owner >= 0, 0.0, AWAY).astype(F32)
             extra = jnp.where(lane_row == n, bias, extra)
-        extra = extra.astype(BF)
         places = places[:4] + [HALO + tile] + places[4:]
-        bases = [p * 128 for p in places]
-        for b in range(2):
-            strips = []
-            for tile_row, pairs in ((0, (1, 2, 3)), (1, (0, 1, 2, 3)), (2, (0, 1, 2))):
-                for pair in pairs:
-                    left, mid, right = (
-                        z_ref[pl.ds(pl.multiple_of(bases[tile_row * 3 + k] + b * 64 + pair * 16, 16), 16), :]
-                        for k in range(3)
-                    )
-                    first, last = ((3, 7), (1, 5))[b]
-                    strips.append(jnp.where(sub < first, left, jnp.where(sub < last, mid, right)))
-            zero = jnp.zeros((16, 128), BF)
-            even = [jnp.where(low_lane, s, zero) for s in strips]
-            odd = [jnp.where(low_lane, zero, s) for s in strips]
-            for a in range(2):
-                quad = 2 * a + b
-                cut = slice(2 * a, 2 * a + 8)
-                held = jnp.concatenate(even[cut] + odd[cut], axis=0)
-                keys = jnp.concatenate([held, key_extra_ref[quad]], axis=1)
-                values = jnp.concatenate([held, ones], axis=1)
-                block = q_ref[pl.ds(pl.multiple_of(tile * 64 + quad * 16, 16), 16), :]
-                query = jnp.concatenate([block[:, h * 128 : h * 128 + 128] for h in range(HEADS)], axis=0)
-                scores = dot_t(jnp.concatenate([query, extra], axis=1), keys)
-                raised = jnp.exp2(scores - jnp.max(scores, axis=1, keepdims=True)).astype(BF)
-                summed = dot(raised, values)
-                part = summed[:, :128]
-                part = (part + pltpu.roll(part, LAT, 1)) / summed[:, 128:]
-                joined = [
-                    jnp.where(low_lane, part[32 * k : 32 * k + 16], part[32 * k + 16 : 32 * k + 32])
-                    for k in range(HEADS // 2)
-                ]
-                u_ref[pl.ds(t * 64 + quad * 16, 16), :] = jnp.concatenate(joined, axis=1).astype(BF)
+        return tile, [p * 128 for p in places], extra.astype(BF)
+
+    def window(bases, b):
+        strips = []
+        for tile_row, pairs in ((0, (1, 2, 3)), (1, (0, 1, 2, 3)), (2, (0, 1, 2))):
+            for pair in pairs:
+                left, mid, right = (
+                    z_ref[pl.ds(pl.multiple_of(bases[tile_row * 3 + k] + b * 64 + pair * 16, 16), 16), :]
+                    for k in range(3)
+                )
+                first, last = ((3, 7), (1, 5))[b]
+                strips.append(jnp.where(sub < first, left, jnp.where(sub < last, mid, right)))
+        return [jnp.where(low_lane, s, zero) for s in strips], [jnp.where(low_lane, zero, s) for s in strips]
+
+    work = {}
+
+    def start(i):
+        t, b, a = i // 4, i // 2 % 2, i % 2
+        quad = 2 * a + b
+        if i % 4 == 0:
+            work["region"] = region(t)
+        tile, bases, extra = work["region"]
+        if a == 0:
+            work["window"] = window(bases, b)
+        even, odd = work["window"]
+        cut = slice(2 * a, 2 * a + 8)
+        held = jnp.concatenate(even[cut] + odd[cut], axis=0)
+        keys = jnp.concatenate([held, key_extra_ref[quad]], axis=1)
+        block = q_ref[pl.ds(pl.multiple_of(tile * 64 + quad * 16, 16), 16), :]
+        query = jnp.concatenate([block[:, h * 128 : h * 128 + 128] for h in range(HEADS)], axis=0)
+        return held, dot_t(jnp.concatenate([query, extra], axis=1), keys)
+
+    def soften(held, scores):
+        raised = jnp.exp2(scores - jnp.max(scores, axis=1, keepdims=True)).astype(BF)
+        return held, raised
+
+    def gather(held, raised):
+        return dot(raised, jnp.concatenate([held, ones], axis=1))
+
+    def finish(i, summed):
+        t, b, a = i // 4, i // 2 % 2, i % 2
+        quad = 2 * a + b
+        part = summed[:, :128]
+        part = (part + pltpu.roll(part, LAT, 1)) / summed[:, 128:]
+        joined = [
+            jnp.where(low_lane, part[32 * k : 32 * k + 16], part[32 * k + 16 : 32 * k + 32])
+            for k in range(HEADS // 2)
+        ]
+        u_ref[pl.ds(t * 64 + quad * 16, 16), :] = jnp.concatenate(joined, axis=1).astype(BF)
+
+    count = GROUP * 4
+    scored, softened, gathered = {}, {}, {}
+    for i in range(count + LAG3):
+        if i < count:
+            scored[i] = start(i)
+        j = i - LAG1
+        if 0 <= j < count:
+            softened[j] = soften(*scored.pop(j))
+        j = i - LAG2
+        if 0 <= j < count:
+            gathered[j] = gather(*softened.pop(j))
+        j = i - LAG3
+        if 0 <= j < count:
+            finish(j, gathered.pop(j))
     placed = dot(back_ref[...], u_ref[...]).astype(BF)
     for n in range(0, D, 512):
         out_ref[:, n : n + 512] = dot(placed, out_mix_ref[:, n : n + 512]).astype(BF)
@@ -191,12 +228,25 @@
 
 
 CHUNK = 512
-
-
-def fold_kernel(
-    embed_ref, gain_ref, wq_ref, wk_ref, wv_ref, wo_ref, mix_ref, out_mix_ref,
-    wq, wk, wv, wo, sems,
+MESH = pl.DeviceIdType.MESH
+
+
+def route_kernel(
+    owner_ref, latents_ref, embed_ref, gain_ref, wq_ref, wk_ref, wv_ref, wo_ref,
+    ext_ref, mix_ref, out_mix_ref,
+    latents, wq, wk, wv, wo, stage, outbox, inbox, own, sems, local_sems,
+    send_sem, recv_sem, halo_send, halo_recv,
 ):
+    devices = lax.axis_size("tile")
+    me = lax.axis_index("tile")
+    edge = HALO * 32
+
+    def load(index, source, target):
+        copy = pltpu.make_async_copy(source, target, local_sems.at[index])
+        copy.start()
+        return copy
+
+    loading = load(0, latents_ref, latents)
     copies = []
     for w, (source, target) in enumerate(((wq_ref, wq), (wk_ref, wk), (wv_ref, wv), (wo_ref, wo))):
         row_count = source.shape[0] // 4
@@ -205,8 +255,55 @@
             copy = pltpu.make_async_copy(source.at[cut], target.at[cut], sems.at[w, c])
             copy.start()
             copies.append(copy)
-    scaled = embed_ref[...].astype(F32) * gain_ref[...]
+
+    barrier = pltpu.get_barrier_semaphore()
+
+    def greet(k, carry):
+        pl.semaphore_signal(barrier, inc=1, device_id={"tile": lax.rem(me + k, devices)}, device_id_type=MESH)
+        return carry
+
+    lax.fori_loop(1, devices, greet, 0)
+
+    slots = owner_ref.shape[0]
+    live = lax.fori_loop(0, slots, lambda j, n: n + jnp.where(owner_ref[j] >= 0, 1, 0), 0)
+    dest = lax.broadcasted_iota(jnp.int32, (devices, slots), 0)
+    slot = lax.broadcasted_iota(jnp.int32, (devices, slots), 1)
+    first = owner_ref[0]
+    chosen = jnp.where(((dest - first) % devices == slot) & (slot < live), 1.0, 0.0).astype(BF)
+    row = lax.broadcasted_iota(jnp.int32, (devices, 128), 0)
+    dead = jnp.where((row - first) % devices < live, 0.0, 512.0)
+    loading.wait()
+    for n in range(0, TILE_VALUES, 512):
+        made = dot(chosen, latents[:, n : n + 512])
+        for k in range(4):
+            stage[pl.ds(n // 128 + k, devices, stride=32), :] = made[:, k * 128 : k * 128 + 128] + dead
+
+    def pack(d, carry):
+        outbox[d] = stage[pl.ds(pl.multiple_of(d * 32, 32), 32), :].astype(BF)
+        return carry
+
+    lax.fori_loop(0, devices, pack, 0)
+    inbox[me] = outbox[me]
+    pl.semaphore_wait(barrier, devices - 1)
+
+    def send(k, carry):
+        target = lax.rem(me + k, devices)
+        pltpu.make_async_remote_copy(
+            src_ref=outbox.at[target], dst_ref=inbox.at[me], send_sem=send_sem, recv_sem=recv_sem,
+            device_id={"tile": target}, device_id_type=MESH,
+        ).start()
+        return carry
+
+    lax.fori_loop(1, devices, send, 0)
+
+    embed = embed_ref[...]
+    scaled = embed.astype(F32) * gain_ref[...]
     stacked = jnp.concatenate(split(scaled), axis=0)
+    twice = jnp.concatenate([embed, embed], axis=0)
+    same = lax.broadcasted_iota(jnp.int32, (128, 128), 0) // LAT == lax.broadcasted_iota(jnp.int32, (128, 128), 1) // LAT
+    gram = jnp.concatenate(split(jnp.where(same, dot_t(twice, twice) * (1.0 / D), 0.0)), axis=1)
+    block = jnp.where(same, 1.0, 0.0).astype(BF)
+    block = jnp.concatenate([block, block], axis=0)
 
     def folded(w, held):
         total = jnp.zeros((2 * LAT, HEADS * HEAD), F32)
@@ -224,6 +321,42 @@
         high, low = split(dot_t(left, jnp.concatenate([right, right], axis=0)) * SCALE)
         mix_ref[:, cut] = jnp.concatenate([high, high, low, low], axis=0)
     value = jnp.concatenate(folded(2, wv), axis=0)
+
+    everyone = pltpu.make_async_remote_copy(
+        src_ref=outbox.at[pl.ds(0, devices - 1)], dst_ref=inbox.at[pl.ds(0, devices - 1)],
+        send_sem=send_sem, recv_sem=recv_sem, device_id={"tile": lax.rem(me + 1, devices)}, device_id_type=MESH,
+    )
+    everyone.wait_recv()
+
+    lane = lax.broadcasted_iota(jnp.int32, (8, 128), 1)
+
+    def rank(source, carry):
+        seen, places = carry
+        lives = inbox[source, 0:16, :].astype(F32)[:8] < 100.0
+        seen = seen + jnp.where(lives, 1, 0)
+        return seen, places + jnp.where(seen <= lane, 1, 0)
+
+    zero = jnp.zeros((8, 128), jnp.int32)
+    _, places = lax.fori_loop(0, devices, rank, (zero, zero))
+    for p in range(TILES):
+        own[pl.ds(p * 32, 32), :] = inbox[jnp.minimum(places[0, p], devices - 1)]
+    held = own[...]
+    tall = dot(held, gram)
+    wide = held.astype(F32)
+    mean = dot(jnp.concatenate(split((tall[:, :128] + tall[:, 128:]) * wide), axis=1), block)
+    own[...] = (wide * lax.rsqrt(jnp.maximum(mean, 0.0) + EPSILON)).astype(BF)
+
+    keep = load(1, own, ext_ref.at[pl.ds(edge, TILES * 32)])
+    halos = []
+    for side, (start, end, step) in enumerate((((TILES - HALO) * 32, 0, 1), (0, edge + TILES * 32, devices - 1))):
+        copy = pltpu.make_async_remote_copy(
+            src_ref=own.at[pl.ds(start, edge)], dst_ref=ext_ref.at[pl.ds(end, edge)],
+            send_sem=halo_send.at[side], recv_sem=halo_recv.at[side],
+            device_id={"tile": lax.rem(me + step, devices)}, device_id_type=MESH,
+        )
+        copy.start()
+        halos.append(copy)
+
     for h in range(HEADS):
         cut = slice(h * HEAD, (h + 1) * HEAD)
         if h % 2 == 0:
@@ -232,50 +365,49 @@
             made = dot(value[:, cut], wo[cut, n : n + 512])
             out_mix_ref[pl.ds(h * LAT, LAT), n : n + 512] = (made[:LAT] + made[LAT:]).astype(BF)
 
-
-def fold(w_embed, norm_gain, w_query, w_key, w_value, w_out):
+    everyone.wait_send()
+    for copy in halos:
+        copy.wait()
+    keep.wait()
+
+
+def route(tile_owner, tile_latents, w_embed, norm_gain, w_query, w_key, w_value, w_out):
+    devices = lax.axis_size("tile")
     vmem = pl.BlockSpec(memory_space=pltpu.VMEM)
     hbm = pl.BlockSpec(memory_space=pl.ANY)
+    smem = pl.BlockSpec(memory_space=pltpu.SMEM)
+    dma = pltpu.SemaphoreType.DMA
     return pl.pallas_call(
-        fold_kernel,
+        route_kernel,
         out_shape=(
+            jax.ShapeDtypeStruct((EXT * 32, 128), BF),
             jax.ShapeDtypeStruct((4 * LAT, HEADS * HEAD), BF),
             jax.ShapeDtypeStruct((HEADS * LAT, D), BF),
         ),
-        in_specs=[vmem, vmem, hbm, hbm, hbm, hbm],
-        out_specs=(vmem, vmem),
-        scratch_shapes=[
-            pltpu.VMEM(w.shape, BF) for w in (w_query, w_key, w_value, w_out)
-        ] + [pltpu.SemaphoreType.DMA((4, 4))],
-        compiler_params=pltpu.CompilerParams(vmem_limit_bytes=48 * 2**20),
+        in_specs=[smem, hbm, vmem, vmem, hbm, hbm, hbm, hbm],
+        out_specs=(hbm, vmem, vmem),
+        scratch_shapes=[pltpu.VMEM(tile_latents.shape, BF)]
+        + [pltpu.VMEM(w.shape, BF) for w in (w_query, w_key, w_value, w_out)]
+        + [
+            pltpu.VMEM((devices * 32, 128), F32),
+            pltpu.VMEM((devices, 32, 128), BF),
+            pltpu.VMEM((devices, 32, 128), BF),
+            pltpu.VMEM((TILES * 32, 128), BF),
+            dma((4, 4)), dma((2,)), dma, dma, dma((2,)), dma((2,)),
+        ],
+        compiler_params=pltpu.CompilerParams(
+            vmem_limit_bytes=48 * 2**20, collective_id=0, has_side_effects=True
+        ),
         cost_estimate=pl.CostEstimate(flops=3 * 10**9, bytes_accessed=2 * 10**7, transcendentals=0),
-        name="fold",
-    )(w_embed, norm_gain.reshape(1, D), w_query, w_key, w_value, w_out)
+        name="route",
+    )(tile_owner, tile_latents, w_embed, norm_gain.reshape(1, D), w_query, w_key, w_value, w_out)
 
 
 def local(
     tile_latents, tile_owner, tile_position, neighbour_owner, neighbour_slot,
     w_embed, norm_gain, w_query, w_key, w_value, w_out,
 ):
-    devices = lax.axis_size("tile")
-    mix, out_mix = fold(w_embed, norm_gain, w_query, w_key, w_value, w_out)
-    chosen = jnp.arange(devices)[:, None] == tile_owner[None, :]
-    outgoing = dot(chosen.astype(BF), tile_latents)
-    dead = ~jnp.any(chosen, axis=1, keepdims=True)
-    outgoing = jnp.where(dead, 512.0, outgoing).astype(BF)
-    arrived = lax.all_to_all(outgoing, "tile", split_axis=0, concat_axis=0, tiled=True)
-    live = arrived[:, 0] < 100.0
-    rank = jnp.cumsum(live.astype(jnp.int32)) - 1
-    taken = (jnp.arange(TILES)[:, None] == rank[None, :]) & live[None, :]
-    owned = dot(taken.astype(BF), arrived).reshape(TILES * 64, LAT)
-    gram = dot_t(w_embed, w_embed) / D
-    mean = jnp.sum(jnp.dot(owned, gram, precision=lax.Precision.HIGHEST) * owned, axis=1, keepdims=True)
-    scaled = (owned * lax.rsqrt(jnp.maximum(mean, 0.0) + EPSILON)).astype(BF).reshape(TILES * 32, 128)
-    up = [(i, (i + 1) % devices) for i in range(devices)]
-    down = [(j, i) for i, j in up]
-    before = lax.ppermute(scaled[(TILES - HALO) * 32 :], "tile", up)
-    after = lax.ppermute(scaled[: HALO * 32], "tile", down)
-    ext = jnp.concatenate([before, scaled, after], axis=0)
+    ext, mix, out_mix = route(tile_owner, tile_latents, w_embed, norm_gain, w_query, w_key, w_value, w_out)
     return attend(neighbour_owner, neighbour_slot, ext, mix, out_mix)
 
 

time: 108 us -> 52.4 us (0.49)
  local copies, waits for them, and re-layouts: 25.7 us -> 4.84 us
  starting transfers between devices: 16.1 us -> 0 us
  waiting for transfers between devices: 8.48 us -> 0 us
  matrix products: 6.54 us -> 0 us
  other arithmetic: 6.44 us -> 0 us
  Pallas kernels: 43.6 us -> 47.2 us
    pallas_call x1, Pallas kernels: 6.9 us -> 28.6 us  [route(): pl.pallas_call(route_kernel, out_shape=(jax.ShapeDtypeStruct((EXT * 32, 1...]
    pallas_call x1, Pallas kernels: 36.7 us -> 18.6 us  [attend(): pl.pallas_call(attend_kernel, grid=(TILES // GROUP,), out_shape=jax.Shape...]
    all_to_all x1 -> x0, starting transfers between devices: 11.8 us -> none  [local(): lax.all_to_all(outgoing, 'tile', split_axis=0, concat_axis=0, tiled=True)]
    dot_general x4 -> x0, matrix products: 6.54 us -> none  [the longest x1 2.32 us: local(): jnp.dot(owned, gram, precision=lax.Precision.HIGHEST) * owned]
    unnamed x23 -> x20, local copies, waits for them, and re-layouts: 10.8 us -> 4.84 us
    ppermute x2 -> x0, waiting for transfers between devices: 5.53 us -> none  [the longest x1 5.53 us: local(): before = lax.ppermute(scaled[(TILES - HALO) * 32:], 'tile', up)]
    slice x3 -> x0, local copies, waits for them, and re-layouts: 5.34 us -> none  [the longest x2 3.58 us: local(): before = lax.ppermute(scaled[(TILES - HALO) * 32:], 'tile', up)]
    ppermute x2 -> x0, starting transfers between devices: 4.31 us -> none  [the longest x1 4.31 us: local(): after = lax.ppermute(scaled[:HALO * 32], 'tile', down)]
  transfers between devices with their start and end apart: 3 -> 0, of which waited for: 2 -> 0; matrix products, arithmetic and copies ran while one was open for 8% -> 0% of each run, Pallas kernels for 6% -> 0%
where the time goes in v2:
time: 52.4 us; the launch traced here: 52.1 us
  Pallas kernels  47.2 us (90%)
  local copies, waits for them, and re-layouts  4.84 us (9%)
    pallas_call x1, Pallas kernels, route(): pl.pallas_call(route_kernel, out_shape=(jax.ShapeDtypeStruct((EXT * 32, 1...  28.6 us
    pallas_call x1, Pallas kernels, attend(): pl.pallas_call(attend_kernel, grid=(TILES // GROUP,), out_shape=jax.Shape...  18.6 us
    unnamed x20, local copies, waits for them, and re-layouts  4.84 us

profile of v2, /device:TPU:0, one launch (start us, length us, event | category | flops | bytes accessed | tf_op | source)
XLA Modules:
  0.0 52.1 jit_solution(9694789591286090915)
XLA Ops:
  0.0 0.8 %copy.16.owner_ref = s32[24,8]{1,0:T(8,128)S(1)} copy(s32[24,8]{0,1:T(8,128)} %param.18) | data formatting | bytes 1536 | tf_op args[3]
  0.8 0.8 %copy.17.slot_ref = s32[24,8]{1,0:T(8,128)S(1)} copy(s32[24,8]{0,1:T(8,128)} %param.19) | data formatting | bytes 1536 | tf_op args[4]
  1.5 0.0 copy-start
  1.5 1.0 %copy-done = bf16[47,4096]{1,0:T(8,128)(2,1)S(1)} copy-done((bf16[47,4096]{1,0:T(8,128)(2,1)S(1)}, bf16[47,4096]{1,0:T(8,128)(2,1)}, u32[]{:S(2)}) %copy-start) | copy-done | bytes 385048
  2.5 0.0 copy-start.1
  2.5 0.9 %copy-done.1 = bf16[64,2048]{1,0:T(8,128)(2,1)S(1)} copy-done((bf16[64,2048]{1,0:T(8,128)(2,1)S(1)}, bf16[64,2048]{1,0:T(8,128)(2,1)}, u32[]{:S(2)}) %copy-start.1) | copy-done | bytes 262168
  3.5 0.0 copy-start.2
  3.5 0.7 %copy-done.2 = f32[2048]{0:T(1024)S(1)} copy-done((f32[2048]{0:T(1024)S(1)}, f32[2048]{0:T(1024)}, u32[]{:S(2)}) %copy-start.2) | copy-done | bytes 8216
  4.2 0.0 copy-start.3
  4.2 0.7 %copy-done.3 = s32[47]{0:T(128)S(1)} copy-done((s32[47]{0:T(128)S(1)}, s32[47]{0:T(128)}, u32[]{:S(2)}) %copy-start.3) | copy-done | bytes 212
  4.8 0.0 copy-start.4
  4.8 0.0 copy-start.5
  4.8 0.0 copy-start.6
  4.8 0.0 copy-start.7
  4.8 0.0 copy-start.8
  4.8 28.6 %route.1 = (bf16[1664,128]{1,0:T(8,128)(2,1)S(1)}, bf16[256,1024]{1,0:T(8,128)(2,1)S(1)}, bf16[512,2048]{1,0:T(8,128)(2,1)S(1)}) custom-call(s32[47]{0:T(128)S(1)} %copy-done.3, bf16[47,4096]{1,0:T(8,128)(2,1)S(1)} %copy-done, bf16[64,2048]{1,0:T(8,128)(2,1)S(1)} %copy-done.1, f32[1,2048]{1,0:T(1,128)S(1)} %bitcast.1, bf16[2048,1024]{1,0:T(8,128)(2,1)} %wq_ref.1, ...), custom_call_target="tpu_custom_call" | custom-call | flops 3000000000 | bytes 20000000 | tf_op jit(solution)/shard_map/route/pallas_call | solution.py:380
  33.4 0.0 copy-done.4
  33.4 0.0 copy-done.5
  33.5 0.0 copy-done.6
  33.5 0.0 copy-done.7
  33.5 0.0 copy-done.8
  33.5 18.6 %attend.1 = bf16[1536,2048]{1,0:T(8,128)(2,1)} custom-call(s32[24,8]{1,0:T(8,128)S(1)} %copy.16.owner_ref, s32[24,8]{1,0:T(8,128)S(1)} %copy.17.slot_ref, bf16[1664,128]{1,0:T(8,128)(2,1)S(1)} %get-tuple-element.8.ext_ref, bf16[256,1024]{1,0:T(8,128)(2,1)S(1)} %get-tuple-element.9.mix_ref, bf16[512,2048]{1,0:T(8,128)(2,1)S(1)} %get-tuple-element.10.out_mix_ref, ...), custom_call_target="tpu_custom_call" | custom-call | flops 8000000000 | bytes 10000000 | tf_op jit(solution)/shard_map/attend/pallas_call | solution.py:213
Async XLA Ops:
  1.5 1.0 %copy-start = (bf16[47,4096]{1,0:T(8,128)(2,1)S(1)}, bf16[47,4096]{1,0:T(8,128)(2,1)}, u32[]{:S(2)}) copy-start(bf16[47,4096]{1,0:T(8,128)(2,1)} %latents_ref.1) | copy-start | bytes 1155076
  2.5 0.9 %copy-start.1 = (bf16[64,2048]{1,0:T(8,128)(2,1)S(1)}, bf16[64,2048]{1,0:T(8,128)(2,1)}, u32[]{:S(2)}) copy-start(bf16[64,2048]{1,0:T(8,128)(2,1)} %embed_ref.1) | copy-start | bytes 786436
  3.5 0.7 %copy-start.2 = (f32[2048]{0:T(1024)S(1)}, f32[2048]{0:T(1024)}, u32[]{:S(2)}) copy-start(f32[2048]{0:T(1024)} %param.21) | copy-start | bytes 24580
  4.2 0.7 %copy-start.3 = (s32[47]{0:T(128)S(1)}, s32[47]{0:T(128)}, u32[]{:S(2)}) copy-start(s32[47]{0:T(128)} %owner_ref.2) | copy-start | bytes 568
  4.8 28.6 %copy-start.4 = (bf16[4,256,128]{2,1,0:T(8,128)(2,1)S(1)}, bf16[4,256,128]{2,1,0:T(8,128)(2,1)}, u32[]{:S(2)}) copy-start(bf16[4,256,128]{2,1,0:T(8,128)(2,1)} %constant.14.clone.key_extra_ref) | copy-start | bytes 786436
  4.8 28.6 %copy-start.5 = (bf16[256,256]{1,0:T(8,128)(2,1)S(1)}, bf16[256,256]{1,0:T(8,128)(2,1)}, u32[]{:S(2)}) copy-start(bf16[256,256]{1,0:T(8,128)(2,1)} %constant.12.clone.back_ref) | copy-start | bytes 393220
  4.8 28.6 %copy-start.6 = (bf16[512,128]{1,0:T(8,128)(2,1)S(1)}, bf16[512,128]{1,0:T(8,128)(2,1)}, u32[]{:S(2)}) copy-start(bf16[512,128]{1,0:T(8,128)(2,1)} %constant.10.clone.spread_ref) | copy-start | bytes 393220
  4.8 28.6 %copy-start.7 = (bf16[256,128]{1,0:T(8,128)(2,1)S(1)}, bf16[256,128]{1,0:T(8,128)(2,1)}, u32[]{:S(2)}) copy-start(bf16[256,128]{1,0:T(8,128)(2,1)} %constant.11.clone.order_ref) | copy-start | bytes 196612
  4.8 28.6 %copy-start.8 = (bf16[128,128]{1,0:T(8,128)(2,1)S(1)}, bf16[128,128]{1,0:T(8,128)(2,1)}, u32[]{:S(2)}) copy-start(bf16[128,128]{1,0:T(8,128)(2,1)} %constant.13.clone.query_extra_ref) | copy-start | bytes 98308

commit v3 on v2

v3 whole, which is shorter than its diff:
```python
import math

import jax
import jax.numpy as jnp
import numpy as np
from jax import lax
from jax.experimental import pallas as pl
from jax.experimental.pallas import tpu as pltpu
from jax.sharding import PartitionSpec as P

D = 2048
HEADS = 8
HEAD = 128
LAT = 64
SIDE = 8
RADIUS = 6
HALO = 14
TILES = 24
TILE_VALUES = 4096
EXT = TILES + 2 * HALO
EPSILON = 1e-06
AWAY = -1e38
GROUP = 4
SCALE = 0.5 * HEAD ** -0.5 * math.log2(math.e)

BF = jnp.bfloat16
F32 = jnp.float32


def place_constants():
    double = np.zeros((2, LAT, 2, 2, LAT), np.float32)
    for p in range(2):
        for k in range(LAT):
            double[p, k, p, :, k] = 1
    double = double.reshape(128, 256)
    spread = np.zeros((GROUP, 2, 8, 8, GROUP, 8, 4), np.float32)
    for t in range(GROUP):
        for form in range(2):
            for r in range(8):
                for s in range(8):
                    spread[t, form, r, s, t, r, (s + 1 + 2 * form) % 4] = 1
    spread = spread.reshape(GROUP * 128, GROUP * 32)
    order = np.zeros((GROUP, 2, 2, 2, 4, 2, GROUP, 8, 4), np.float32)
    back = np.zeros((GROUP, 8, 8, GROUP, 2, 2, 2, 4, 2), np.float32)
    for t in range(GROUP):
        for a in range(2):
            for b in range(2):
                for p in range(2):
                    for r in range(4):
                        for c in range(2):
                            order[t, a, b, p, r, c, t, 4 * a + r, 2 * b + c] = 1
                            back[t, 4 * a + r, 4 * b + 2 * c + p, t, a, b, p, r, c] = 1
    order = order.reshape(GROUP * 64, GROUP * 32)
    back = back.reshape(GROUP * 64, GROUP * 64)
    query_extra = np.zeros((2, 4, 2, 128), np.float32)
    for p in range(2):
        for r in range(4):
            for c in range(2):
                query_extra[p, r, c, 8 + r] = 1
                query_extra[p, r, c, 12 + 2 * c + p] = 1
    query_extra = query_extra.reshape(16, 128)
    key_extra = np.zeros((2, 2, 2, 16, 8, 128), np.float32)
    for a in range(2):
        for b in range(2):
            for p in range(2):
                for row in range(16):
                    for s in range(8):
                        col = 2 * s + p
                        tile_row = (4 * a - 6 + row) // 8 + 1
                        tile_col = (4 * b - 6 + col) // 8 + 1
                        region = tile_row * 3 + tile_col
                        lane = key_extra[a, b, p, row, s]
                        if region != 4:
                            lane[region - (region > 4)] = 1
                        for i in range(4):
                            lane[8 + i] = 0 if i <= row <= i + 2 * RADIUS else AWAY
                            lane[12 + i] = 0 if i <= col <= i + 2 * RADIUS else AWAY
    key_extra = key_extra.reshape(1024, 128)
    stack = lambda x: np.concatenate([x[:, :128], x[:, 128:]], axis=0)
    moving = np.concatenate([stack(double), spread, order], axis=0).astype(jnp.bfloat16)
    fixed = np.concatenate([stack(back), query_extra, key_extra], axis=0).astype(jnp.bfloat16)
    return moving, fixed


def split(x):
    high = x.astype(BF)
    low = (x - high.astype(F32)).astype(BF)
    return high, low


def dot(a, b):
    return jnp.dot(a, b, preferred_element_type=F32)


def dot_t(a, b):
    return lax.dot_general(a, b, (((1,), (1,)), ((), ())), preferred_element_type=F32)


LAG1, LAG2, LAG3 = 2, 4, 6
OUT_AT = 3


def attend_kernel(
    owner_ref, slot_ref, z_ref, q_ref, out_mix_ref, fixed_ref, out_ref, u_ref, bias_ref, placed_ref, made_ref, sems,
):
    me = lax.axis_index("tile")
    low_lane = lax.broadcasted_iota(jnp.int32, (16, 128), 1) < LAT

    lane = lax.broadcasted_iota(jnp.int32, (16, 128), 1)
    sides = []
    for t in range(TILES):
        side = fixed_ref[pl.ds(512, 16), :].astype(F32)
        for n in range(8):
            side = jnp.where(lane == n, jnp.where(owner_ref[n, t] >= 0, 0.0, AWAY).astype(F32), side)
        sides.append(side.astype(BF))
    bias_ref[...] = dot_t(jnp.concatenate(sides, axis=0), fixed_ref[pl.ds(528, 1024), :])
    sub = lax.broadcasted_iota(jnp.int32, (16, 128), 0) % 8
    ones = jnp.ones((256, 128), BF)

    rows = GROUP * 64
    last = TILES // GROUP

    def place():
        placed_ref[...] = dot(jnp.concatenate([fixed_ref[0:256, :], fixed_ref[256:512, :]], axis=1), u_ref[...]).astype(BF)

    def copy_out(g):
        slot = g % 2
        return pltpu.make_async_copy(
            made_ref.at[slot], out_ref.at[pl.ds(pl.multiple_of(g * rows, rows), rows)], sems.at[slot]
        )

    def body(step, carry):
        @pl.when(step >= 3)
        def _():
            copy_out(step - 3).wait()

        place()
        slot = (step + 1) % 2

        def project(n):
            made_ref[slot, :, n * 512 : n * 512 + 512] = dot(
                placed_ref[...], out_mix_ref[:, n * 512 : n * 512 + 512]
            ).astype(BF)

        def region(t):
            tile = step * GROUP + t
            places = []
            for n in range(8):
                owner = owner_ref[n, tile]
                place = HALO + (owner - me) * TILES + slot_ref[n, tile]
                places.append(jnp.where(owner >= 0, place, HALO + tile))
            places = places[:4] + [HALO + tile] + places[4:]
            return tile, [p * 128 for p in places]

        def window(bases, b):
            first, last = ((3, 7), (1, 5))[b]
            sides = []
            for p in range(2):
                strips = []
                for tile_row, pairs in ((0, (1, 2, 3)), (1, (0, 1, 2, 3)), (2, (0, 1, 2))):
                    for pair in pairs:
                        left, mid, right = (
                            z_ref[p, pl.ds(pl.multiple_of(bases[tile_row * 3 + k] + b * 64 + pair * 16, 16), 16), :]
                            for k in range(3)
                        )
                        strips.append(jnp.where(sub < first, left, jnp.where(sub < last, mid, right)))
                sides.append(strips)
            return sides

        work = {}

        def start(i):
            t, b, a = i // 4, i // 2 % 2, i % 2
            quad = 2 * a + b
            if i % 4 == 0:
                work["region"] = region(t)
            tile, bases = work["region"]
            if a == 0:
                work["window"] = window(bases, b)
            even, odd = work["window"]
            cut = slice(2 * a, 2 * a + 8)
            held = jnp.concatenate(even[cut] + odd[cut], axis=0)
            block = q_ref[pl.ds(pl.multiple_of(tile * 64 + quad * 16, 16), 16), :]
            query = jnp.concatenate([block[:, h * 128 : h * 128 + 128] for h in range(HEADS)], axis=0)
            bias = bias_ref[pl.ds(pl.multiple_of(tile * 16, 16), 16), quad * 256 : quad * 256 + 256]
            return held, dot_t(query, held) + jnp.concatenate([bias] * HEADS, axis=0)

        def soften(held, scores):
            raised = jnp.exp2(scores - jnp.max(scores, axis=1, keepdims=True)).astype(BF)
            return held, raised

        def gather(held, raised):
            return dot(raised, jnp.concatenate([held, ones], axis=1))

        def finish(i, summed):
            t, b, a = i // 4, i // 2 % 2, i % 2
            quad = 2 * a + b
            part = summed[:, :128] / summed[:, 128:]
            joined = [
                jnp.where(low_lane, part[32 * k : 32 * k + 16], part[32 * k + 16 : 32 * k + 32])
                for k in range(HEADS // 2)
            ]
            u_ref[pl.ds(t * 64 + quad * 16, 16), :] = jnp.concatenate(joined, axis=1).astype(BF)

        count = GROUP * 4
        scored, softened, gathered = {}, {}, {}
        for i in range(count + LAG3):
            if i < count:
                scored[i] = start(i)
            if i % 4 == OUT_AT and i < count:
                project(i // 4)
            j = i - LAG1
            if 0 <= j < count:
                softened[j] = soften(*scored.pop(j))
            j = i - LAG2
            if 0 <= j < count:
                gathered[j] = gather(*softened.pop(j))
            j = i - LAG3
            if 0 <= j < count:
                finish(j, gathered.pop(j))

        @pl.when(step >= 1)
        def _():
            copy_out(step - 1).start()

        return carry

    u_ref[...] = jnp.zeros(u_ref.shape, BF)
    lax.fori_loop(0, last, body, 0)
    copy_out(last - 3).wait()
    place()
    for n in range(0, D, 512):
        made_ref[(last - 1) % 2, :, n : n + 512] = dot(placed_ref[...], out_mix_ref[:, n : n + 512]).astype(BF)
    copy_out(last - 1).start()
    copy_out(last - 2).wait()
    copy_out(last - 1).wait()


def attend(owner, slot, z, q, out_mix, fixed):
    smem = pl.BlockSpec(memory_space=pltpu.SMEM)
    vmem = pl.BlockSpec(memory_space=pltpu.VMEM)
    rows = GROUP * 64
    return pl.pallas_call(
        attend_kernel,
        out_shape=jax.ShapeDtypeStruct((TILES * 64, D), BF),
        in_specs=[smem, smem] + [vmem] * 4,
        out_specs=pl.BlockSpec(memory_space=pl.ANY),
        scratch_shapes=[
            pltpu.VMEM((rows, HEADS * LAT), BF),
            pltpu.VMEM((TILES * 16, 1024), F32),
            pltpu.VMEM((rows, HEADS * LAT), BF),
            pltpu.VMEM((2, rows, D), BF),
            pltpu.SemaphoreType.DMA((2,)),
        ],
        compiler_params=pltpu.CompilerParams(vmem_limit_bytes=24 * 2**20),
        cost_estimate=pl.CostEstimate(flops=8 * 10**9, bytes_accessed=10**7, transcendentals=3 * 10**6),
        name="attend",
    )(owner.T, slot.T, z, q, out_mix, fixed)


CHUNK = 512
MESH = pl.DeviceIdType.MESH


def route_kernel(
    owner_in, latents_ref, embed_in, gain_in, wq_ref, wk_ref, wv_ref, wo_ref,
    moving_in,
    z_ref, q_ref, out_mix_ref,
    latents, wq, wk, wv, wo, owner_ref, embed_ref, gain_ref, moving, mix_ref, stage, outbox, inbox, ext, sems, local_sems,
    send_sem, recv_sem, halo_send, halo_recv,
):
    devices = lax.axis_size("tile")
    me = lax.axis_index("tile")
    edge = HALO * 32

    def load(index, source, target):
        copy = pltpu.make_async_copy(source, target, local_sems.at[index])
        copy.start()
        return copy

    owners = load(0, owner_in, owner_ref)
    loading = load(1, latents_ref, latents)
    parameters = [load(2, embed_in, embed_ref), load(3, gain_in, gain_ref), load(4, moving_in, moving)]
    copies = []
    for w, (source, target) in enumerate(((wq_ref, wq), (wk_ref, wk), (wv_ref, wv), (wo_ref, wo))):
        row_count = source.shape[0] // 4
        for c in range(4):
            cut = pl.ds(c * row_count, row_count)
            copy = pltpu.make_async_copy(source.at[cut], target.at[cut], sems.at[w, c])
            copy.start()
            copies.append(copy)

    barrier = pltpu.get_barrier_semaphore()

    def greet(k, carry):
        pl.semaphore_signal(barrier, inc=1, device_id={"tile": lax.rem(me + k, devices)}, device_id_type=MESH)
        return carry

    lax.fori_loop(1, devices, greet, 0)

    owners.wait()
    slots = owner_ref.shape[0]
    live = lax.fori_loop(0, slots, lambda j, n: n + jnp.where(owner_ref[j] >= 0, 1, 0), 0)
    dest = lax.broadcasted_iota(jnp.int32, (devices, slots), 0)
    slot = lax.broadcasted_iota(jnp.int32, (devices, slots), 1)
    first = owner_ref[0]
    chosen = jnp.where(((dest - first) % devices == slot) & (slot < live), 1.0, 0.0).astype(BF)
    row = lax.broadcasted_iota(jnp.int32, (devices, 128), 0)
    dead = jnp.where((row - first) % devices < live, 0.0, 512.0)
    loading.wait()
    for n in range(0, TILE_VALUES, 512):
        made = dot(chosen, latents[:, n : n + 512])
        for k in range(4):
            stage[pl.ds(n // 128 + k, devices, stride=32), :] = made[:, k * 128 : k * 128 + 128] + dead

    def pack(d, carry):
        outbox[d] = stage[pl.ds(pl.multiple_of(d * 32, 32), 32), :].astype(BF)
        return carry

    lax.fori_loop(0, devices, pack, 0)
    inbox[me] = outbox[me]
    pl.semaphore_wait(barrier, devices - 1)

    def send(k, carry):
        target = lax.rem(me + k, devices)
        pltpu.make_async_remote_copy(
            src_ref=outbox.at[target], dst_ref=inbox.at[me], send_sem=send_sem, recv_sem=recv_sem,
            device_id={"tile": target}, device_id_type=MESH,
        ).start()
        return carry

    lax.fori_loop(1, devices, send, 0)

    for copy in parameters:
        copy.wait()
    embed = embed_ref[...]
    scaled = embed.astype(F32) * gain_ref[...]
    stacked = jnp.concatenate(split(scaled), axis=0)
    twice = jnp.concatenate([embed, embed], axis=0)
    same = lax.broadcasted_iota(jnp.int32, (128, 128), 0) // LAT == lax.broadcasted_iota(jnp.int32, (128, 128), 1) // LAT
    gram = jnp.concatenate(split(jnp.where(same, dot_t(twice, twice) * (1.0 / D), 0.0)), axis=1)
    block = jnp.where(same, 1.0, 0.0).astype(BF)
    block = jnp.concatenate([block, block], axis=0)

    def folded(w, held):
        total = jnp.zeros((2 * LAT, HEADS * HEAD), F32)
        for c in range(4):
            copies[w * 4 + c].wait()
            total += dot(stacked[:, c * CHUNK : (c + 1) * CHUNK], held[pl.ds(c * CHUNK, CHUNK), :])
        return split(total[:LAT] + total[LAT:])

    query_high, query_low = folded(0, wq)
    key_high, key_low = folded(1, wk)
    for h in range(HEADS):
        cut = slice(h * HEAD, (h + 1) * HEAD)
        left = jnp.concatenate([query_high[:, cut], query_low[:, cut], query_high[:, cut]], axis=1)
        right = jnp.concatenate([key_high[:, cut], key_high[:, cut], key_low[:, cut]], axis=1)
        high, low = split(dot_t(left, jnp.concatenate([right, right], axis=0)) * SCALE)
        mix_ref[:, cut] = jnp.concatenate([high, high, low, low], axis=0)
    value = jnp.concatenate(folded(2, wv), axis=0)

    for h in range(HEADS):
        cut = slice(h * HEAD, (h + 1) * HEAD)
        if h % 2 == 0:
            copies[12 + h // 2].wait()
        for n in range(0, D, 512):
            made = dot(value[:, cut], wo[cut, n : n + 512])
            out_mix_ref[pl.ds(h * LAT, LAT), n : n + 512] = (made[:LAT] + made[LAT:]).astype(BF)

    everyone = pltpu.make_async_remote_copy(
        src_ref=outbox.at[pl.ds(0, devices - 1)], dst_ref=inbox.at[pl.ds(0, devices - 1)],
        send_sem=send_sem, recv_sem=recv_sem, device_id={"tile": lax.rem(me + 1, devices)}, device_id_type=MESH,
    )
    everyone.wait_recv()

    lane = lax.broadcasted_iota(jnp.int32, (8, 128), 1)

    def rank(source, carry):
        seen, places = carry
        lives = inbox[source, 0:16, :].astype(F32)[:8] < 100.0
        seen = seen + jnp.where(lives, 1, 0)
        return seen, places + jnp.where(seen <= lane, 1, 0)

    zero = jnp.zeros((8, 128), jnp.int32)
    _, places = lax.fori_loop(0, devices, rank, (zero, zero))
    for p in range(TILES):
        ext[pl.ds(edge + p * 32, 32), :] = inbox[jnp.minimum(places[0, p], devices - 1)]
    mine = pl.ds(edge, TILES * 32)
    held = ext[mine, :]
    tall = dot(held, gram)
    wide = held.astype(F32)
    mean = dot(jnp.concatenate(split((tall[:, :128] + tall[:, 128:]) * wide), axis=1), block)
    ext[mine, :] = (wide * lax.rsqrt(jnp.maximum(mean, 0.0) + EPSILON)).astype(BF)

    halos = []
    for side, (start, end, step) in enumerate(((TILES * 32, 0, 1), (edge, edge + TILES * 32, devices - 1))):
        copy = pltpu.make_async_remote_copy(
            src_ref=ext.at[pl.ds(start, edge)], dst_ref=ext.at[pl.ds(end, edge)],
            send_sem=halo_send.at[side], recv_sem=halo_recv.at[side],
            device_id={"tile": lax.rem(me + step, devices)}, device_id_type=MESH,
        )
        copy.start()
        halos.append(copy)

    rows = GROUP * 32
    order = moving[pl.ds(768, 256), :]
    double = jnp.concatenate([moving[0:128, :], moving[128:256, :]], axis=1)
    spread = moving[pl.ds(256, 512), :]
    parity = (lax.broadcasted_iota(jnp.int32, (GROUP * 64, 128), 0) // 8) % 2
    half = lax.broadcasted_iota(jnp.int32, (GROUP * 64, 128), 1) // LAT
    keep = (parity == half).astype(F32)
    for g in range(TILES // GROUP):
        picked = (dot(order, ext[pl.ds(edge + g * rows, rows), :]) * keep).astype(BF)
        both = jnp.concatenate([picked, picked], axis=1)
        q_ref[pl.ds(g * GROUP * 64, GROUP * 64), :] = dot(both, mix_ref[...]).astype(BF)

    def spread_out(first):
        pair = dot(ext[pl.ds(first * 32, rows), :], double).astype(BF)
        made = dot(spread, pair).astype(BF)
        for p in range(2):
            z_ref[p, pl.ds(first * 128, GROUP * 128), :] = made[:, p * 128 : p * 128 + 128]

    for g in range(TILES // GROUP):
        spread_out(HALO + g * GROUP)
    everyone.wait_send()
    for copy in halos:
        copy.wait()
    for start in (0, HALO + TILES):
        for first in (0, 4, 8, HALO - GROUP):
            spread_out(start + first)


def route(tile_owner, tile_latents, w_embed, norm_gain, w_query, w_key, w_value, w_out, moving):
    devices = lax.axis_size("tile")
    vmem = pl.BlockSpec(memory_space=pltpu.VMEM)
    hbm = pl.BlockSpec(memory_space=pltpu.HBM)
    dma = pltpu.SemaphoreType.DMA
    return pl.pallas_call(
        route_kernel,
        out_shape=(
            jax.ShapeDtypeStruct((2, EXT * 128, 128), BF),
            jax.ShapeDtypeStruct((TILES * 64, HEADS * HEAD), BF),
            jax.ShapeDtypeStruct((HEADS * LAT, D), BF),
        ),
        in_specs=[hbm] * 9,
        out_specs=(vmem, vmem, vmem),
        scratch_shapes=[pltpu.VMEM(tile_latents.shape, BF)]
        + [pltpu.VMEM(w.shape, BF) for w in (w_query, w_key, w_value, w_out)]
        + [
            pltpu.SMEM(tile_owner.shape, jnp.int32),
            pltpu.VMEM(w_embed.shape, BF),
            pltpu.VMEM((1, D), F32),
            pltpu.VMEM(moving.shape, BF),
            pltpu.VMEM((4 * LAT, HEADS * HEAD), BF),
            pltpu.VMEM((devices * 32, 128), F32),
            pltpu.VMEM((devices, 32, 128), BF),
            pltpu.VMEM((devices, 32, 128), BF),
            pltpu.VMEM((EXT * 32, 128), BF),
            dma((4, 4)), dma((5,)), dma, dma, dma((2,)), dma((2,)),
        ],
        compiler_params=pltpu.CompilerParams(
            vmem_limit_bytes=40 * 2**20, collective_id=0, has_side_effects=True
        ),
        cost_estimate=pl.CostEstimate(flops=3 * 10**9, bytes_accessed=2 * 10**7, transcendentals=0),
        name="route",
    )(
        *[
            pltpu.with_memory_space_constraint(x, pltpu.HBM)
            for x in (
                tile_owner, tile_latents, w_embed, norm_gain.reshape(1, D), w_query, w_key, w_value, w_out, moving,
            )
        ],
    )


def local(
    tile_latents, tile_owner, tile_position, neighbour_owner, neighbour_slot,
    w_embed, norm_gain, w_query, w_key, w_value, w_out,
):
    moving, fixed = (jnp.asarray(c) for c in place_constants())
    z, q, out_mix = route(tile_owner, tile_latents, w_embed, norm_gain, w_query, w_key, w_value, w_out, moving)
    return attend(neighbour_owner, neighbour_slot, z, q, out_mix, fixed)


def solution(mesh):
    both = P(("dp", "tile"), None)
    flat = P(("dp", "tile"))
    return jax.shard_map(
        local,
        mesh=mesh,
        in_specs=(both, flat, flat, both, both, P(), P(), P(), P(), P(), P()),
        out_specs=both,
        check_vma=False,
    )
```

time: 52.4 us -> 40.4 us (0.77)
  Pallas kernels: 47.2 us -> 40.3 us
  local copies, waits for them, and re-layouts: 4.84 us -> 0.01 us
    pallas_call x2, Pallas kernels: 47.2 us -> 40.3 us  [the longest x1 29 us: route(): pl.pallas_call(route_kernel, out_shape=(jax.ShapeDtypeStruct((2, EXT * 12...]
    unnamed x20 -> x6, local copies, waits for them, and re-layouts: 4.84 us -> 0.01 us
where the time goes in v3:
time: 40.4 us; the launch traced here: 40.3 us
  Pallas kernels  40.3 us (100%)
    pallas_call x1, Pallas kernels, route(): pl.pallas_call(route_kernel, out_shape=(jax.ShapeDtypeStruct((2, EXT * 12...  29 us
    pallas_call x1, Pallas kernels, attend(): pl.pallas_call(attend_kernel, out_shape=jax.ShapeDtypeStruct((TILES * 64,...  11.3 us

profile of v3, /device:TPU:0, one launch (start us, length us, event | category | flops | bytes accessed | tf_op | source)
XLA Modules:
  0.0 40.3 jit_solution(17540141770251562733)
XLA Ops:
  0.0 0.0 copy-start
  0.0 0.0 copy-start.1
  0.0 0.0 copy-start.2
  0.0 29.0 %route.1 = (bf16[2,6656,128]{2,1,0:T(8,128)(2,1)S(1)}, bf16[1536,1024]{1,0:T(8,128)(2,1)S(1)}, bf16[512,2048]{1,0:T(8,128)(2,1)S(1)}) custom-call(s32[47]{0:T(128)} %owner_in.1, bf16[47,4096]{1,0:T(8,128)(2,1)} %latents_ref.1, bf16[64,2048]{1,0:T(8,128)(2,1)} %embed_in.1, f32[1,2048]{1,0:T(1,128)} %bitcast.5, bf16[2048,1024]{1,0:T(8,128)(2,1)} %wq_ref.1, ...), custom_call_target="tpu_custom_call" | custom-call | flops 3000000000 | bytes 20000000 | tf_op jit(solution)/shard_map/route/pallas_call | solution.py:438
  29.1 0.0 copy-done
  29.1 0.0 copy-done.1
  29.1 0.0 copy-done.2
  29.1 11.3 %attend.1 = bf16[1536,2048]{1,0:T(8,128)(2,1)} custom-call(s32[8,24]{1,0:T(8,128)S(1)} %bitcast.3, s32[8,24]{1,0:T(8,128)S(1)} %bitcast.4, bf16[2,6656,128]{2,1,0:T(8,128)(2,1)S(1)} %get-tuple-element.8.z_ref, bf16[1536,1024]{1,0:T(8,128)(2,1)S(1)} %get-tuple-element.9.q_ref, bf16[512,2048]{1,0:T(8,128)(2,1)S(1)} %get-tuple-element.10.out_mix_ref, ...), custom_call_target="tpu_custom_call" | custom-call | flops 8000000000 | bytes 10000000 | tf_op jit(solution)/shard_map/attend/pallas_call | solution.py:243
Async XLA Ops:
  0.0 29.1 %copy-start = (s32[24,8]{0,1:T(8,128)S(1)}, s32[24,8]{0,1:T(8,128)}, u32[]{:S(2)}) copy-start(s32[24,8]{0,1:T(8,128)} %param.15) | copy-start | bytes 2308
  0.0 29.1 %copy-start.1 = (s32[24,8]{0,1:T(8,128)S(1)}, s32[24,8]{0,1:T(8,128)}, u32[]{:S(2)}) copy-start(s32[24,8]{0,1:T(8,128)} %param.16) | copy-start | bytes 2308
  0.0 29.1 %copy-start.2 = (bf16[1552,128]{1,0:T(8,128)(2,1)S(1)}, bf16[1552,128]{1,0:T(8,128)(2,1)}, u32[]{:S(2)}) copy-start(bf16[1552,128]{1,0:T(8,128)(2,1)} %constant.5.clone.fixed_ref) | copy-start | bytes 1191940

commit v4 on v3

--- a/solution.py
+++ b/solution.py
@@ -77,8 +77,8 @@
                             lane[12 + i] = 0 if i <= col <= i + 2 * RADIUS else AWAY
     key_extra = key_extra.reshape(1024, 128)
     stack = lambda x: np.concatenate([x[:, :128], x[:, 128:]], axis=0)
-    moving = np.concatenate([stack(double), spread, order], axis=0).astype(jnp.bfloat16)
-    fixed = np.concatenate([stack(back), query_extra, key_extra], axis=0).astype(jnp.bfloat16)
+    moving = np.concatenate([stack(double), spread, order, query_extra, key_extra], axis=0).astype(jnp.bfloat16)
+    fixed = stack(back).astype(jnp.bfloat16)
     return moving, fixed
 
 
@@ -101,19 +101,11 @@
 
 
 def attend_kernel(
-    owner_ref, slot_ref, z_ref, q_ref, out_mix_ref, fixed_ref, out_ref, u_ref, bias_ref, placed_ref, made_ref, sems,
+    owner_ref, slot_ref, z_ref, q_ref, bias_ref, out_mix_ref, fixed_ref, out_ref, u_ref, placed_ref, made_ref, sems, piece_sems,
 ):
     me = lax.axis_index("tile")
     low_lane = lax.broadcasted_iota(jnp.int32, (16, 128), 1) < LAT
 
-    lane = lax.broadcasted_iota(jnp.int32, (16, 128), 1)
-    sides = []
-    for t in range(TILES):
-        side = fixed_ref[pl.ds(512, 16), :].astype(F32)
-        for n in range(8):
-            side = jnp.where(lane == n, jnp.where(owner_ref[n, t] >= 0, 0.0, AWAY).astype(F32), side)
-        sides.append(side.astype(BF))
-    bias_ref[...] = dot_t(jnp.concatenate(sides, axis=0), fixed_ref[pl.ds(528, 1024), :])
     sub = lax.broadcasted_iota(jnp.int32, (16, 128), 0) % 8
     ones = jnp.ones((256, 128), BF)
 
@@ -229,33 +221,41 @@
     lax.fori_loop(0, last, body, 0)
     copy_out(last - 3).wait()
     place()
-    for n in range(0, D, 512):
-        made_ref[(last - 1) % 2, :, n : n + 512] = dot(placed_ref[...], out_mix_ref[:, n : n + 512]).astype(BF)
-    copy_out(last - 1).start()
+    pieces = []
+    for k in range(4):
+        cut = slice(k * 512, k * 512 + 512)
+        made_ref[(last - 1) % 2, :, cut] = dot(placed_ref[...], out_mix_ref[:, cut]).astype(BF)
+        piece = pltpu.make_async_copy(
+            made_ref.at[(last - 1) % 2, :, pl.ds(k * 512, 512)],
+            out_ref.at[pl.ds((last - 1) * rows, rows), pl.ds(k * 512, 512)], piece_sems.at[k],
+        )
+        piece.start()
+        pieces.append(piece)
     copy_out(last - 2).wait()
-    copy_out(last - 1).wait()
-
-
-def attend(owner, slot, z, q, out_mix, fixed):
+    for piece in pieces:
+        piece.wait()
+
+
+def attend(owner, slot, z, q, bias, out_mix, fixed):
     smem = pl.BlockSpec(memory_space=pltpu.SMEM)
     vmem = pl.BlockSpec(memory_space=pltpu.VMEM)
     rows = GROUP * 64
     return pl.pallas_call(
         attend_kernel,
         out_shape=jax.ShapeDtypeStruct((TILES * 64, D), BF),
-        in_specs=[smem, smem] + [vmem] * 4,
+        in_specs=[smem, smem] + [vmem] * 5,
         out_specs=pl.BlockSpec(memory_space=pl.ANY),
         scratch_shapes=[
             pltpu.VMEM((rows, HEADS * LAT), BF),
-            pltpu.VMEM((TILES * 16, 1024), F32),
             pltpu.VMEM((rows, HEADS * LAT), BF),
             pltpu.VMEM((2, rows, D), BF),
             pltpu.SemaphoreType.DMA((2,)),
+            pltpu.SemaphoreType.DMA((4,)),
         ],
         compiler_params=pltpu.CompilerParams(vmem_limit_bytes=24 * 2**20),
         cost_estimate=pl.CostEstimate(flops=8 * 10**9, bytes_accessed=10**7, transcendentals=3 * 10**6),
         name="attend",
-    )(owner.T, slot.T, z, q, out_mix, fixed)
+    )(owner.T, slot.T, z, q, bias, out_mix, fixed)
 
 
 CHUNK = 512
@@ -264,9 +264,9 @@
 
 def route_kernel(
     owner_in, latents_ref, embed_in, gain_in, wq_ref, wk_ref, wv_ref, wo_ref,
-    moving_in,
-    z_ref, q_ref, out_mix_ref,
-    latents, wq, wk, wv, wo, owner_ref, embed_ref, gain_ref, moving, mix_ref, stage, outbox, inbox, ext, sems, local_sems,
+    moving_in, around_in,
+    z_ref, q_ref, bias_ref, out_mix_ref,
+    latents, wq, wk, wv, wo, owner_ref, embed_ref, gain_ref, moving, around, mix_ref, stage, outbox, inbox, ext, sems, local_sems,
     send_sem, recv_sem, halo_send, halo_recv,
 ):
     devices = lax.axis_size("tile")
@@ -280,7 +280,16 @@
 
     owners = load(0, owner_in, owner_ref)
     loading = load(1, latents_ref, latents)
-    parameters = [load(2, embed_in, embed_ref), load(3, gain_in, gain_ref), load(4, moving_in, moving)]
+
+    barrier = pltpu.get_barrier_semaphore()
+
+    def greet(k, carry):
+        pl.semaphore_signal(barrier, inc=1, device_id={"tile": lax.rem(me + k, devices)}, device_id_type=MESH)
+        return carry
+
+    lax.fori_loop(1, devices, greet, 0)
+
+    parameters = [load(2, embed_in, embed_ref), load(3, gain_in, gain_ref), load(4, moving_in, moving), load(5, around_in, around)]
     copies = []
     for w, (source, target) in enumerate(((wq_ref, wq), (wk_ref, wk), (wv_ref, wv), (wo_ref, wo))):
         row_count = source.shape[0] // 4
@@ -289,14 +298,6 @@
             copy = pltpu.make_async_copy(source.at[cut], target.at[cut], sems.at[w, c])
             copy.start()
             copies.append(copy)
-
-    barrier = pltpu.get_barrier_semaphore()
-
-    def greet(k, carry):
-        pl.semaphore_signal(barrier, inc=1, device_id={"tile": lax.rem(me + k, devices)}, device_id_type=MESH)
-        return carry
-
-    lax.fori_loop(1, devices, greet, 0)
 
     owners.wait()
     slots = owner_ref.shape[0]
@@ -317,7 +318,7 @@
         outbox[d] = stage[pl.ds(pl.multiple_of(d * 32, 32), 32), :].astype(BF)
         return carry
 
-    lax.fori_loop(0, devices, pack, 0)
+    lax.fori_loop(0, devices, pack, 0, unroll=8)
     inbox[me] = outbox[me]
     pl.semaphore_wait(barrier, devices - 1)
 
@@ -367,6 +368,14 @@
             made = dot(value[:, cut], wo[cut, n : n + 512])
             out_mix_ref[pl.ds(h * LAT, LAT), n : n + 512] = (made[:LAT] + made[LAT:]).astype(BF)
 
+    extra_lane = lax.broadcasted_iota(jnp.int32, (16, 128), 1)
+    sides = []
+    for t in range(TILES):
+        side = moving[pl.ds(1024, 16), :].astype(F32)
+        for n in range(8):
+            side = jnp.where(extra_lane == n, jnp.where(around[n, t] >= 0, 0.0, AWAY).astype(F32), side)
+        sides.append(side.astype(BF))
+    bias_ref[...] = dot_t(jnp.concatenate(sides, axis=0), moving[pl.ds(1040, 1024), :])
     everyone = pltpu.make_async_remote_copy(
         src_ref=outbox.at[pl.ds(0, devices - 1)], dst_ref=inbox.at[pl.ds(0, devices - 1)],
         send_sem=send_sem, recv_sem=recv_sem, device_id={"tile": lax.rem(me + 1, devices)}, device_id_type=MESH,
@@ -382,7 +391,7 @@
         return seen, places + jnp.where(seen <= lane, 1, 0)
 
     zero = jnp.zeros((8, 128), jnp.int32)
-    _, places = lax.fori_loop(0, devices, rank, (zero, zero))
+    _, places = lax.fori_loop(0, devices, rank, (zero, zero), unroll=8)
     for p in range(TILES):
         ext[pl.ds(edge + p * 32, 32), :] = inbox[jnp.minimum(places[0, p], devices - 1)]
     mine = pl.ds(edge, TILES * 32)
@@ -392,15 +401,31 @@
     mean = dot(jnp.concatenate(split((tall[:, :128] + tall[:, 128:]) * wide), axis=1), block)
     ext[mine, :] = (wide * lax.rsqrt(jnp.maximum(mean, 0.0) + EPSILON)).astype(BF)
 
-    halos = []
-    for side, (start, end, step) in enumerate(((TILES * 32, 0, 1), (edge, edge + TILES * 32, devices - 1))):
-        copy = pltpu.make_async_remote_copy(
+    last = devices - 1
+
+    def halo(side):
+        start, end, partner = ((TILES * 32, 0, me + 1), (edge, edge + TILES * 32, me - 1))[side]
+        return pltpu.make_async_remote_copy(
             src_ref=ext.at[pl.ds(start, edge)], dst_ref=ext.at[pl.ds(end, edge)],
             send_sem=halo_send.at[side], recv_sem=halo_recv.at[side],
-            device_id={"tile": lax.rem(me + step, devices)}, device_id_type=MESH,
+            device_id={"tile": lax.rem(partner + devices, devices)}, device_id_type=MESH,
         )
-        copy.start()
-        halos.append(copy)
+
+    @pl.when(me < last)
+    def _():
+        halo(0).start()
+
+    @pl.when(me > 0)
+    def _():
+        halo(1).start()
+
+    @pl.when(me == 0)
+    def _():
+        ext[pl.ds(0, edge), :] = jnp.zeros((edge, 128), BF)
+
+    @pl.when(me == last)
+    def _():
+        ext[pl.ds(edge + TILES * 32, edge), :] = jnp.zeros((edge, 128), BF)
 
     rows = GROUP * 32
     order = moving[pl.ds(768, 256), :]
@@ -423,14 +448,23 @@
     for g in range(TILES // GROUP):
         spread_out(HALO + g * GROUP)
     everyone.wait_send()
-    for copy in halos:
-        copy.wait()
+
+    @pl.when(me < last)
+    def _():
+        halo(0).wait_send()
+        halo(1).wait_recv()
+
+    @pl.when(me > 0)
+    def _():
+        halo(1).wait_send()
+        halo(0).wait_recv()
+
     for start in (0, HALO + TILES):
         for first in (0, 4, 8, HALO - GROUP):
             spread_out(start + first)
 
 
-def route(tile_owner, tile_latents, w_embed, norm_gain, w_query, w_key, w_value, w_out, moving):
+def route(tile_owner, tile_latents, w_embed, norm_gain, w_query, w_key, w_value, w_out, moving, around):
     devices = lax.axis_size("tile")
     vmem = pl.BlockSpec(memory_space=pltpu.VMEM)
     hbm = pl.BlockSpec(memory_space=pltpu.HBM)
@@ -440,10 +474,11 @@
         out_shape=(
             jax.ShapeDtypeStruct((2, EXT * 128, 128), BF),
             jax.ShapeDtypeStruct((TILES * 64, HEADS * HEAD), BF),
+            jax.ShapeDtypeStruct((TILES * 16, 1024), F32),
             jax.ShapeDtypeStruct((HEADS * LAT, D), BF),
         ),
-        in_specs=[hbm] * 9,
-        out_specs=(vmem, vmem, vmem),
+        in_specs=[hbm] * 10,
+        out_specs=(vmem, vmem, vmem, vmem),
         scratch_shapes=[pltpu.VMEM(tile_latents.shape, BF)]
         + [pltpu.VMEM(w.shape, BF) for w in (w_query, w_key, w_value, w_out)]
         + [
@@ -451,12 +486,13 @@
             pltpu.VMEM(w_embed.shape, BF),
             pltpu.VMEM((1, D), F32),
             pltpu.VMEM(moving.shape, BF),
+            pltpu.SMEM(around.shape, jnp.int32),
             pltpu.VMEM((4 * LAT, HEADS * HEAD), BF),
             pltpu.VMEM((devices * 32, 128), F32),
             pltpu.VMEM((devices, 32, 128), BF),
             pltpu.VMEM((devices, 32, 128), BF),
             pltpu.VMEM((EXT * 32, 128), BF),
-            dma((4, 4)), dma((5,)), dma, dma, dma((2,)), dma((2,)),
+            dma((4, 4)), dma((6,)), dma, dma, dma((2,)), dma((2,)),
         ],
         compiler_params=pltpu.CompilerParams(
             vmem_limit_bytes=40 * 2**20, collective_id=0, has_side_effects=True
@@ -468,6 +504,7 @@
             pltpu.with_memory_space_constraint(x, pltpu.HBM)
             for x in (
                 tile_owner, tile_latents, w_embed, norm_gain.reshape(1, D), w_query, w_key, w_value, w_out, moving,
+                around,
             )
         ],
     )
@@ -478,8 +515,10 @@
     w_embed, norm_gain, w_query, w_key, w_value, w_out,
 ):
     moving, fixed = (jnp.asarray(c) for c in place_constants())
-    z, q, out_mix = route(tile_owner, tile_latents, w_embed, norm_gain, w_query, w_key, w_value, w_out, moving)
-    return attend(neighbour_owner, neighbour_slot, z, q, out_mix, fixed)
+    z, q, bias, out_mix = route(
+        tile_owner, tile_latents, w_embed, norm_gain, w_query, w_key, w_value, w_out, moving, neighbour_owner.T
+    )
+    return attend(neighbour_owner, neighbour_slot, z, q, bias, out_mix, fixed)
 
 
 def solution(mesh):

time: 40.4 us -> 37.4 us (0.926)
  the two profiles are of different devices: /device:TPU:0 before, /device:TPU:8 now
where the time goes in v4:
time: 37.4 us; the launch traced here: 37.3 us
  Pallas kernels  37.2 us (99%)
    pallas_call x1, Pallas kernels, route(): pl.pallas_call(route_kernel, out_shape=(jax.ShapeDtypeStruct((2, EXT * 12...  26.6 us
    pallas_call x1, Pallas kernels, attend(): pl.pallas_call(attend_kernel, out_shape=jax.ShapeDtypeStruct((TILES * 64,...  10.6 us

profile of v4, /device:TPU:8, one launch (start us, length us, event | category | flops | bytes accessed | tf_op | source)
XLA Modules:
  0.0 37.3 jit_solution(7746731267223132577)
XLA Ops:
  0.0 0.0 copy-start
  0.0 0.0 copy-start.1
  0.0 0.0 copy-start.2
  0.0 26.6 %route.1 = (bf16[2,6656,128]{2,1,0:T(8,128)(2,1)S(1)}, bf16[1536,1024]{1,0:T(8,128)(2,1)S(1)}, f32[384,1024]{1,0:T(8,128)S(1)}, bf16[512,2048]{1,0:T(8,128)(2,1)S(1)}) custom-call(s32[47]{0:T(128)} %owner_in.1, bf16[47,4096]{1,0:T(8,128)(2,1)} %latents_ref.1, bf16[64,2048]{1,0:T(8,128)(2,1)} %embed_in.1, f32[1,2048]{1,0:T(1,128)} %bitcast.6, ...), custom_call_target="tpu_custom_call" | custom-call | flops 3000000000 | bytes 20000000 | tf_op jit(solution)/shard_map/route/pallas_call | solution.py:472
  26.6 0.0 copy-done
  26.7 0.0 copy-done.1
  26.7 0.0 copy-done.2
  26.7 10.6 %attend.1 = bf16[1536,2048]{1,0:T(8,128)(2,1)} custom-call(s32[8,24]{1,0:T(8,128)S(1)} %bitcast.4, s32[8,24]{1,0:T(8,128)S(1)} %bitcast.5, bf16[2,6656,128]{2,1,0:T(8,128)(2,1)S(1)} %get-tuple-element.9.z_ref, bf16[1536,1024]{1,0:T(8,128)(2,1)S(1)} %get-tuple-element.10.q_ref, f32[384,1024]{1,0:T(8,128)S(1)} %get-tuple-element.11.bias_ref, ...), custom_call_target="tpu_custom_call" | custom-call | flops 8000000000 | bytes 10000000 | tf_op jit(solution)/shard_map/attend/pallas_call | solution.py:243
Async XLA Ops:
  0.0 26.6 %copy-start = (s32[24,8]{0,1:T(8,128)S(1)}, s32[24,8]{0,1:T(8,128)}, u32[]{:S(2)}) copy-start(s32[24,8]{0,1:T(8,128)} %param.15) | copy-start | bytes 2308
  0.0 26.7 %copy-start.1 = (s32[24,8]{0,1:T(8,128)S(1)}, s32[24,8]{0,1:T(8,128)}, u32[]{:S(2)}) copy-start(s32[24,8]{0,1:T(8,128)} %param.16) | copy-start | bytes 2308
  0.0 26.7 %copy-start.2 = (bf16[512,128]{1,0:T(8,128)(2,1)S(1)}, bf16[512,128]{1,0:T(8,128)(2,1)}, u32[]{:S(2)}) copy-start(bf16[512,128]{1,0:T(8,128)(2,1)} %constant.5.clone.fixed_ref) | copy-start | bytes 393220

commit v5 on v4

--- a/solution.py
+++ b/solution.py
@@ -118,7 +118,7 @@
     def copy_out(g):
         slot = g % 2
         return pltpu.make_async_copy(
-            made_ref.at[slot], out_ref.at[pl.ds(pl.multiple_of(g * rows, rows), rows)], sems.at[slot]
+            made_ref.at[slot], out_ref.at[pl.ds(g * rows, rows)], sems.at[slot]
         )
 
     def body(step, carry):
@@ -126,7 +126,8 @@
         def _():
             copy_out(step - 3).wait()
 
-        place()
+        if step:
+            place()
         slot = (step + 1) % 2
 
         def project(n):
@@ -172,9 +173,9 @@
             even, odd = work["window"]
             cut = slice(2 * a, 2 * a + 8)
             held = jnp.concatenate(even[cut] + odd[cut], axis=0)
-            block = q_ref[pl.ds(pl.multiple_of(tile * 64 + quad * 16, 16), 16), :]
+            block = q_ref[pl.ds(tile * 64 + quad * 16, 16), :]
             query = jnp.concatenate([block[:, h * 128 : h * 128 + 128] for h in range(HEADS)], axis=0)
-            bias = bias_ref[pl.ds(pl.multiple_of(tile * 16, 16), 16), quad * 256 : quad * 256 + 256]
+            bias = bias_ref[pl.ds(tile * 16, 16), quad * 256 : quad * 256 + 256]
             return held, dot_t(query, held) + jnp.concatenate([bias] * HEADS, axis=0)
 
         def soften(held, scores):
@@ -199,7 +200,7 @@
         for i in range(count + LAG3):
             if i < count:
                 scored[i] = start(i)
-            if i % 4 == OUT_AT and i < count:
+            if i % 4 == OUT_AT and i < count and step:
                 project(i // 4)
             j = i - LAG1
             if 0 <= j < count:
@@ -218,7 +219,8 @@
         return carry
 
     u_ref[...] = jnp.zeros(u_ref.shape, BF)
-    lax.fori_loop(0, last, body, 0)
+    for step in range(last):
+        body(step, 0)
     copy_out(last - 3).wait()
     place()
     pieces = []
@@ -358,24 +360,6 @@
         right = jnp.concatenate([key_high[:, cut], key_high[:, cut], key_low[:, cut]], axis=1)
         high, low = split(dot_t(left, jnp.concatenate([right, right], axis=0)) * SCALE)
         mix_ref[:, cut] = jnp.concatenate([high, high, low, low], axis=0)
-    value = jnp.concatenate(folded(2, wv), axis=0)
-
-    for h in range(HEADS):
-        cut = slice(h * HEAD, (h + 1) * HEAD)
-        if h % 2 == 0:
-            copies[12 + h // 2].wait()
-        for n in range(0, D, 512):
-            made = dot(value[:, cut], wo[cut, n : n + 512])
-            out_mix_ref[pl.ds(h * LAT, LAT), n : n + 512] = (made[:LAT] + made[LAT:]).astype(BF)
-
-    extra_lane = lax.broadcasted_iota(jnp.int32, (16, 128), 1)
-    sides = []
-    for t in range(TILES):
-        side = moving[pl.ds(1024, 16), :].astype(F32)
-        for n in range(8):
-            side = jnp.where(extra_lane == n, jnp.where(around[n, t] >= 0, 0.0, AWAY).astype(F32), side)
-        sides.append(side.astype(BF))
-    bias_ref[...] = dot_t(jnp.concatenate(sides, axis=0), moving[pl.ds(1040, 1024), :])
     everyone = pltpu.make_async_remote_copy(
         src_ref=outbox.at[pl.ds(0, devices - 1)], dst_ref=inbox.at[pl.ds(0, devices - 1)],
         send_sem=send_sem, recv_sem=recv_sem, device_id={"tile": lax.rem(me + 1, devices)}, device_id_type=MESH,
@@ -447,6 +431,24 @@
 
     for g in range(TILES // GROUP):
         spread_out(HALO + g * GROUP)
+    value = jnp.concatenate(folded(2, wv), axis=0)
+
+    for h in range(HEADS):
+        cut = slice(h * HEAD, (h + 1) * HEAD)
+        if h % 2 == 0:
+            copies[12 + h // 2].wait()
+        for n in range(0, D, 512):
+            made = dot(value[:, cut], wo[cut, n : n + 512])
+            out_mix_ref[pl.ds(h * LAT, LAT), n : n + 512] = (made[:LAT] + made[LAT:]).astype(BF)
+
+    extra_lane = lax.broadcasted_iota(jnp.int32, (16, 128), 1)
+    sides = []
+    for t in range(TILES):
+        side = moving[pl.ds(1024, 16), :].astype(F32)
+        for n in range(8):
+            side = jnp.where(extra_lane == n, jnp.where(around[n, t] >= 0, 0.0, AWAY).astype(F32), side)
+        sides.append(side.astype(BF))
+    bias_ref[...] = dot_t(jnp.concatenate(sides, axis=0), moving[pl.ds(1040, 1024), :])
     everyone.wait_send()
 
     @pl.when(me < last)

time: 37.4 us -> 36.9 us (0.987)
  the two profiles are of different devices: /device:TPU:8 before, /device:TPU:0 now
where the time goes in v5:
time: 36.9 us; the launch traced here: 36.5 us
  Pallas kernels  36.3 us (98%)
    pallas_call x1, Pallas kernels, route(): pl.pallas_call(route_kernel, out_shape=(jax.ShapeDtypeStruct((2, EXT * 12...  26.3 us
    pallas_call x1, Pallas kernels, attend(): pl.pallas_call(attend_kernel, out_shape=jax.ShapeDtypeStruct((TILES * 64,...  9.97 us

profile of v5, /device:TPU:0, one launch (start us, length us, event | category | flops | bytes accessed | tf_op | source)
XLA Modules:
  0.0 36.5 jit_solution(8121621681585617975)
XLA Ops:
  0.0 0.0 copy-start
  0.0 0.0 copy-start.1
  0.0 0.0 copy-start.2
  0.0 26.3 %route.1 = (bf16[2,6656,128]{2,1,0:T(8,128)(2,1)S(1)}, bf16[1536,1024]{1,0:T(8,128)(2,1)S(1)}, f32[384,1024]{1,0:T(8,128)S(1)}, bf16[512,2048]{1,0:T(8,128)(2,1)S(1)}) custom-call(s32[47]{0:T(128)} %owner_in.1, bf16[47,4096]{1,0:T(8,128)(2,1)} %latents_ref.1, bf16[64,2048]{1,0:T(8,128)(2,1)} %embed_in.1, f32[1,2048]{1,0:T(1,128)} %bitcast.6, ...), custom_call_target="tpu_custom_call" | custom-call | flops 3000000000 | bytes 20000000 | tf_op jit(solution)/shard_map/route/pallas_call | solution.py:474
  26.3 0.0 copy-done
  26.4 0.0 copy-done.1
  26.4 0.0 copy-done.2
  26.4 10.0 %attend.1 = bf16[1536,2048]{1,0:T(8,128)(2,1)} custom-call(s32[8,24]{1,0:T(8,128)S(1)} %bitcast.4, s32[8,24]{1,0:T(8,128)S(1)} %bitcast.5, bf16[2,6656,128]{2,1,0:T(8,128)(2,1)S(1)} %get-tuple-element.9.z_ref, bf16[1536,1024]{1,0:T(8,128)(2,1)S(1)} %get-tuple-element.10.q_ref, f32[384,1024]{1,0:T(8,128)S(1)} %get-tuple-element.11.bias_ref, ...), custom_call_target="tpu_custom_call" | custom-call | flops 8000000000 | bytes 10000000 | tf_op jit(solution)/shard_map/attend/pallas_call | solution.py:245
Async XLA Ops:
  0.0 26.3 %copy-start = (s32[24,8]{0,1:T(8,128)S(1)}, s32[24,8]{0,1:T(8,128)}, u32[]{:S(2)}) copy-start(s32[24,8]{0,1:T(8,128)} %param.15) | copy-start | bytes 2308
  0.0 26.4 %copy-start.1 = (s32[24,8]{0,1:T(8,128)S(1)}, s32[24,8]{0,1:T(8,128)}, u32[]{:S(2)}) copy-start(s32[24,8]{0,1:T(8,128)} %param.16) | copy-start | bytes 2308
  0.0 26.4 %copy-start.2 = (bf16[512,128]{1,0:T(8,128)(2,1)S(1)}, bf16[512,128]{1,0:T(8,128)(2,1)}, u32[]{:S(2)}) copy-start(bf16[512,128]{1,0:T(8,128)(2,1)} %constant.5.clone.fixed_ref) | copy-start | bytes 393220

commit v6 on v5

--- a/solution.py
+++ b/solution.py
@@ -289,7 +289,7 @@
         pl.semaphore_signal(barrier, inc=1, device_id={"tile": lax.rem(me + k, devices)}, device_id_type=MESH)
         return carry
 
-    lax.fori_loop(1, devices, greet, 0)
+    lax.fori_loop(1, devices, greet, 0, unroll=7)
 
     parameters = [load(2, embed_in, embed_ref), load(3, gain_in, gain_ref), load(4, moving_in, moving), load(5, around_in, around)]
     copies = []
@@ -332,7 +332,7 @@
         ).start()
         return carry
 
-    lax.fori_loop(1, devices, send, 0)
+    lax.fori_loop(1, devices, send, 0, unroll=7)
 
     for copy in parameters:
         copy.wait()
@@ -375,7 +375,7 @@
         return seen, places + jnp.where(seen <= lane, 1, 0)
 
     zero = jnp.zeros((8, 128), jnp.int32)
-    _, places = lax.fori_loop(0, devices, rank, (zero, zero), unroll=8)
+    _, places = lax.fori_loop(0, devices, rank, (zero, zero), unroll=16)
     for p in range(TILES):
         ext[pl.ds(edge + p * 32, 32), :] = inbox[jnp.minimum(places[0, p], devices - 1)]
     mine = pl.ds(edge, TILES * 32)

time: 36.9 us -> 36.7 us (level)
  Pallas kernels: 36.3 us -> 35.9 us
where the time goes in v6:
time: 36.7 us; the launch traced here: 36.1 us
  Pallas kernels  35.9 us (98%)
    pallas_call x1, Pallas kernels, route(): pl.pallas_call(route_kernel, out_shape=(jax.ShapeDtypeStruct((2, EXT * 12...  26 us
    pallas_call x1, Pallas kernels, attend(): pl.pallas_call(attend_kernel, out_shape=jax.ShapeDtypeStruct((TILES * 64,...  9.97 us

profile of v6, /device:TPU:0, one launch (start us, length us, event | category | flops | bytes accessed | tf_op | source)
XLA Modules:
  0.0 36.1 jit_solution(11929988849070736916)
XLA Ops:
  0.0 0.0 copy-start
  0.0 0.0 copy-start.1
  0.0 0.0 copy-start.2
  0.0 26.0 %route.1 = (bf16[2,6656,128]{2,1,0:T(8,128)(2,1)S(1)}, bf16[1536,1024]{1,0:T(8,128)(2,1)S(1)}, f32[384,1024]{1,0:T(8,128)S(1)}, bf16[512,2048]{1,0:T(8,128)(2,1)S(1)}) custom-call(s32[47]{0:T(128)} %owner_in.1, bf16[47,4096]{1,0:T(8,128)(2,1)} %latents_ref.1, bf16[64,2048]{1,0:T(8,128)(2,1)} %embed_in.1, f32[1,2048]{1,0:T(1,128)} %bitcast.6, ...), custom_call_target="tpu_custom_call" | custom-call | flops 3000000000 | bytes 20000000 | tf_op jit(solution)/shard_map/route/pallas_call | solution.py:474
  26.0 0.0 copy-done
  26.0 0.0 copy-done.1
  26.0 0.0 copy-done.2
  26.0 10.0 %attend.1 = bf16[1536,2048]{1,0:T(8,128)(2,1)} custom-call(s32[8,24]{1,0:T(8,128)S(1)} %bitcast.4, s32[8,24]{1,0:T(8,128)S(1)} %bitcast.5, bf16[2,6656,128]{2,1,0:T(8,128)(2,1)S(1)} %get-tuple-element.9.z_ref, bf16[1536,1024]{1,0:T(8,128)(2,1)S(1)} %get-tuple-element.10.q_ref, f32[384,1024]{1,0:T(8,128)S(1)} %get-tuple-element.11.bias_ref, ...), custom_call_target="tpu_custom_call" | custom-call | flops 8000000000 | bytes 10000000 | tf_op jit(solution)/shard_map/attend/pallas_call | solution.py:245
Async XLA Ops:
  0.0 26.0 %copy-start = (s32[24,8]{0,1:T(8,128)S(1)}, s32[24,8]{0,1:T(8,128)}, u32[]{:S(2)}) copy-start(s32[24,8]{0,1:T(8,128)} %param.15) | copy-start | bytes 2308
  0.0 26.0 %copy-start.1 = (s32[24,8]{0,1:T(8,128)S(1)}, s32[24,8]{0,1:T(8,128)}, u32[]{:S(2)}) copy-start(s32[24,8]{0,1:T(8,128)} %param.16) | copy-start | bytes 2308
  0.0 26.0 %copy-start.2 = (bf16[512,128]{1,0:T(8,128)(2,1)S(1)}, bf16[512,128]{1,0:T(8,128)(2,1)}, u32[]{:S(2)}) copy-start(bf16[512,128]{1,0:T(8,128)(2,1)} %constant.5.clone.fixed_ref) | copy-start | bytes 393220
